TPU v7x, 128 devices: a whole 4x4x4 slice. The times are simulated.
128 devices in a mesh: ctx: 64 (over z, x, y), head: 2 (over core).
Axes of the slice: x: 4, y: 4, z: 4, core: 2. Of those that a mesh axis runs over, the one named last changes fastest.
Arguments:
- query_rows: bfloat16 [65536, 2048], P('ctx', 'head'), may hold values from -6 to 6
- key_rows: bfloat16 [65536, 2048], P('ctx', 'head'), may hold values from -6 to 6
- value_rows: bfloat16 [65536, 2048], P('ctx', 'head'), may hold values from -6 to 6
- out_grad: bfloat16 [65536, 2048], P('ctx', 'head'), may hold values from -6 to 6
- out_weight: bfloat16 [2048, 2048], P('head'), may hold values from -0.125 to 0.125
Outputs:
- query_gradient: bfloat16 [65536, 2048], P('ctx', 'head')
- key_gradient: bfloat16 [65536, 2048], P('ctx', 'head')
- value_gradient: bfloat16 [65536, 2048], P('ctx', 'head')
All inputs are finite; a program needn't handle non-finite values.
Results may differ from a plain program's by a relative error of at most 0.005.
Values may be sent and summed in bfloat16 or wider, within the bound.
No kernel may reach another device: no remote copies, remote signals or barrier semaphores. Data moves between devices by JAX's collectives and lax.ppermute only.
A program may use at most 192 MiB of HBM per device.

v0:
```python
import math

import jax
import jax.numpy as jnp
from jax import lax
from jax.sharding import PartitionSpec as P

HEAD_WIDTH_SIZE = 128
BLOCK = 512


def carried_in(value, axis, join, neutral, backward):
    count, mine = (lax.axis_size(axis), lax.axis_index(axis))
    pieces = lax.all_gather(value, axis)
    if backward:
        pieces = pieces[::-1]
        mine = count - 1 - mine
    subtotal = jnp.full_like(value, 0) + jnp.asarray(neutral, value.dtype)

    def step(position, subtotal):
        longer = join(subtotal, pieces[position])
        return jnp.where(position < mine, longer, subtotal)

    return lax.fori_loop(0, count - 1, step, subtotal)


def plus_state(earlier, later):
    return earlier + later


def per_device(query_rows, key_rows, value_rows, out_grad, out_weight):
    length = query_rows.shape[0]
    blocks = length // BLOCK
    heads_here = query_rows.shape[1] // HEAD_WIDTH_SIZE
    scale_factor = 1.0 / math.sqrt(HEAD_WIDTH_SIZE * length * lax.axis_size("ctx"))
    full_grad = lax.all_gather(out_grad, "head", axis=1, tiled=True)
    head_grad = lax.dot_general(
        full_grad, out_weight, (((1,), (1,)), ((), ())), preferred_element_type=jnp.float32
    ).astype(jnp.bfloat16)
    shape_blocks = (blocks, BLOCK, heads_here, HEAD_WIDTH_SIZE)
    qblock = query_rows.reshape(shape_blocks)
    kblock = key_rows.reshape(shape_blocks)
    vblock = value_rows.reshape(shape_blocks)
    gblock = head_grad.reshape(shape_blocks)
    key_state = jnp.einsum("bthk,bthv->bhkv", kblock, vblock, preferred_element_type=jnp.float32)
    grad_state = jnp.einsum("bthk,bthv->bhkv", qblock, gblock, preferred_element_type=jnp.float32)
    own_keys = jnp.sum(key_state, axis=0)
    own_grads = jnp.sum(grad_state, axis=0)
    zeros_state = jnp.zeros_like(own_keys)
    before = carried_in(own_keys, "ctx", plus_state, zeros_state, False)
    suffix = carried_in(own_grads, "ctx", plus_state, zeros_state, True)
    position = jnp.arange(BLOCK)
    causal = (position[:, None] >= position[None, :])[None]
    maximal_precision_mode = lax.Precision.HIGHEST

    def one_block(carry, parts):
        key_running_carry, grad_carry = carry
        query_part, key_segment, value_segment, gradient_segment, key_step, grad_step = parts
        gradient_remainder = grad_carry - grad_step
        scores = jnp.einsum(
            "thk,shk->hts", query_part, key_segment, preferred_element_type=jnp.float32
        )
        probs_low = jnp.where(causal, scale_factor * scores, 0.0).astype(jnp.bfloat16)
        dscore = jnp.einsum(
            "thv,shv->hts", gradient_segment, value_segment, preferred_element_type=jnp.float32
        )
        weight_low = jnp.where(causal, scale_factor * dscore, 0.0).astype(jnp.bfloat16)
        query_out = jnp.einsum(
            "hts,shk->thk", weight_low, key_segment, preferred_element_type=jnp.float32
        ) + scale_factor * jnp.einsum(
            "nxb,xcb->nxc",
            gradient_segment.astype(jnp.float32),
            key_running_carry,
            precision=maximal_precision_mode,
        )
        key_out = jnp.einsum(
            "hts,thk->shk", weight_low, query_part, preferred_element_type=jnp.float32
        ) + scale_factor * jnp.einsum(
            "jlw,lyw->jly",
            value_segment.astype(jnp.float32),
            gradient_remainder,
            precision=maximal_precision_mode,
        )
        value_out = jnp.einsum(
            "hts,thv->shv", probs_low, gradient_segment, preferred_element_type=jnp.float32
        ) + scale_factor * jnp.einsum(
            "yiw,iwd->yid",
            key_segment.astype(jnp.float32),
            gradient_remainder,
            precision=maximal_precision_mode,
        )
        results = (
            query_out.astype(jnp.bfloat16),
            key_out.astype(jnp.bfloat16),
            value_out.astype(jnp.bfloat16),
        )
        return ((key_running_carry + key_step, gradient_remainder), results)

    start_carry = (before, suffix + own_grads)
    unused, outputs = lax.scan(
        one_block, start_carry, (qblock, kblock, vblock, gblock, key_state, grad_state)
    )
    query_gradient, key_gradient, value_gradient = outputs
    width_here = heads_here * HEAD_WIDTH_SIZE
    return (
        query_gradient.reshape(length, width_here),
        key_gradient.reshape(length, width_here),
        value_gradient.reshape(length, width_here),
    )


def solution(mesh):
    placed = (
        P("ctx", "head"),
        P("ctx", "head"),
        P("ctx", "head"),
        P("ctx", "head"),
        P("head", None),
    )
    return jax.shard_map(
        per_device,
        mesh=mesh,
        in_specs=placed,
        out_specs=(P("ctx", "head"), P("ctx", "head"), P("ctx", "head")),
        check_vma=False,
    )
```

profile of v0, /device:TPU:1, one launch (start us, length us, event | category | flops | bytes accessed | tf_op | source)
XLA Modules:
  0.0 543.9 jit_solution(6198814563043809536)
XLA Ops:
  10.7 3.0 copy.41
  13.7 3.0 copy.69
  21.7 8.0 %all-gather.6.cloned.1.call-done = bf16[1024,2048]{1,0:T(8,128)(2,1)} async-done(((bf16[1024,1024]{1,0:T(8,128)(2,1)}), bf16[1024,2048]{1,0:T(8,128)(2,1)}) %all-gather.6.cloned.1.call-update) | async-done | bytes 4194320 | tf_op jit(solution)/shard_map/all_gather | solution.py:36
  29.7 8.0 %convert_bitcast_fusion = bf16[128,8,8,128]{3,1,2,0:T(8,128)(2,1)S(1)} fusion(bf16[1024,2048]{1,0:T(8,128)(2,1)} %all-gather.6.cloned.1.call-done, bf16[1024,2048]{1,0:T(8,128)(2,1)} %param.15), kind=kOutput, calls=%fused_computation.54 | convolution fusion | flops 4296015872 | bytes 10485760 | tf_op jit(solution)/shard_map/dot_general | solution.py:37
  39.7 3.7 fusion.49
  44.4 3.5 copy.42
  47.9 146.4 %all-gather.8.cloned.1.call-done = f32[512,128,128]{2,1,0:T(8,128)} async-done(((f32[8,128,128]{2,1,0:T(8,128)}), f32[512,128,128]{2,1,0:T(8,128)}) %all-gather.8.cloned.1.call-update) | async-done | bytes 33554448 | tf_op jit(solution)/shard_map/all_gather | solution.py:14
  194.3 79.8 %while.49 = (s32[]{:T(128)}, f32[8,128,128]{2,1,0:T(8,128)S(1)}, s32[]{:T(128)}, f32[64,8,128,128]{3,2,1,0:T(8,128)}, s32[]{:T(128)}, /*index=5*/s32[]{:T(128)}) while((s32[]{:T(128)}, f32[8,128,128]{2,1,0:T(8,128)S(1)}, s32[]{:T(128)}, f32[64,8,128,128]{3,2,1,0:T(8,128)}, s32[]{:T(128)}, /*index=5*/s32[]{:T(128)}) %tuple.108), condition=%wide.region_2.3_spmd.clone, body=%wide.region_1.0_spmd.clone.sunk | while | flops 393220 | bytes 1572957 | solution.py:24
  274.1 83.5 %all-gather.10.cloned.1.call-done = f32[512,128,128]{2,1,0:T(8,128)} async-done(((f32[8,128,128]{2,1,0:T(8,128)}), f32[512,128,128]{2,1,0:T(8,128)}) %all-gather.10.cloned.1.call-update) | async-done | bytes 33554448 | tf_op jit(solution)/shard_map/all_gather | solution.py:14
  357.7 23.0 %rev.3 = f32[64,8,128,128]{3,2,1,0:T(8,128)} reverse(f32[64,8,128,128]{3,2,1,0:T(8,128)} %bitcast.142), dimensions={0} | reverse | bytes 67108864 | tf_op jit(solution)/shard_map/rev | solution.py:16
  380.7 78.8 %while.50 = (s32[]{:T(128)}, f32[8,128,128]{2,1,0:T(8,128)S(1)}, s32[]{:T(128)}, f32[64,8,128,128]{3,2,1,0:T(8,128)}, s32[]{:T(128)}, /*index=5*/s32[]{:T(128)}) while((s32[]{:T(128)}, f32[8,128,128]{2,1,0:T(8,128)S(1)}, s32[]{:T(128)}, f32[64,8,128,128]{3,2,1,0:T(8,128)}, s32[]{:T(128)}, /*index=5*/s32[]{:T(128)}) %tuple.94), condition=%wide.region_5.6_spmd.clone, body=%wide.region_4.5_spmd.clone.sunk | while | flops 393220 | bytes 1572957 | solution.py:24
  459.8 70.5 %while.48 = (s32[]{:T(128)}, f32[8,128,128]{2,1,0:T(8,128)S(1)}, f32[8,128,128]{1,2,0:T(8,128)S(1)}, bf16[2,512,8,128]{3,2,1,0:T(8,128)(2,1)}, bf16[2,512,8,128]...) while((s32[]{:T(128)}, f32[8,128,128]{2,1,0:T(8,128)S(1)}, ...), condition=%wide.region_7.8_spmd.clone.clone, body=%wide.region_6.7_spmd.clone.clone.sunk | while | flops 5118099456 | bytes 105123632 | solution.py:100
  461.2 4.8 select_convert_fusion.6
  466.8 3.0 fusion.94
  470.0 3.4 fusion.95
  475.1 4.9 fusion.92
  480.0 4.0 fusion.93
  496.4 4.9 select_convert_fusion.6
  502.1 3.0 fusion.94
  505.2 3.4 fusion.95
  510.3 4.9 fusion.92
  515.2 4.0 fusion.93
  530.3 3.7 copy.98
  534.0 3.3 copy_bitcast_fusion.4
  (206 shorter events, 197.1 us)
Async XLA Ops:
  7.2 1.6 copy-start.9
  7.2 22.5 %all-gather.6.cloned.1.call-start = ((), (), s32[]{:S(2)}) async-start(), calls=%async_computation | async-start | bytes 6291456 | tf_op jit(solution)/shard_map/all_gather | solution.py:36
  7.9 186.4 %all-gather.8.cloned.1.call-start = ((), (), s32[]{:S(2)}) async-start(), calls=%async_computation.1 | async-start | bytes 34078720 | tf_op jit(solution)/shard_map/all_gather | solution.py:14
  13.7 3.0 copy-start.3
  16.7 2.7 copy-start.6
  19.4 338.3 %all-gather.10.cloned.1.call-start = ((), (), s32[]{:S(2)}) async-start(), calls=%async_computation.2 | async-start | bytes 34078720 | tf_op jit(solution)/shard_map/all_gather | solution.py:14
  21.7 18.0 %copy-start.4 = (bf16[128,8,8,128]{3,2,1,0:T(8,128)(2,1)}, bf16[128,8,8,128]{3,2,1,0:T(8,128)(2,1)S(1)}, u32[]{:S(2)}) copy-start(bf16[128,8,8,128]{3,2,1,0:T(8,128)(2,1)S(1)} %copy.71) | copy-start | bytes 6291460
  461.1 5.0 copy-start.1
  461.2 4.9 copy-start.5
  466.8 3.0 copy-start.8
  485.7 2.9 copy-start
  488.7 2.8 copy-start.2
  493.3 1.6 copy-start.7
  496.3 5.0 copy-start.1
  496.4 4.9 copy-start.5
  502.1 3.0 copy-start.8
  521.0 2.9 copy-start
  523.9 2.8 copy-start.2
  528.6 1.6 copy-start.7
  530.3 3.7 copy-start.10
  530.3 3.7 copy-start.11
Sparse Core Ops, SparseCore 0:
  9.7 20.0 all-gather.5
  32.6 161.7 all-gather.7
  197.2 160.4 all-gather.9
where the time goes:
time: 551 us; the launch traced here: 544 us
  waiting for transfers between devices  239 us (43%)
  other arithmetic  156 us (28%)
  local copies, waits for them, and re-layouts  69.1 us (13%)
  matrix products  62.4 us (11%)
  between operations  13.9 us (3%)
    all_gather x2, waiting for transfers between devices, carried_in(): pieces = lax.all_gather(value, axis)  230 us
    select_n x126, other arithmetic, step(): return jnp.where(position < mine, longer, subtotal)  156 us
    rev x1, local copies, waits for them, and re-layouts, carried_in(): pieces = pieces[::-1]  23 us
    unnamed x17, local copies, waits for them, and re-layouts  13.6 us
    dynamic_update_slice x10, local copies, waits for them, and re-layouts, per_device(): lax.scan(one_block, start_carry, (qblock, kblock, vblock, gblock, key_sta...  13.4 us
  transfers between devices with their start and end apart: 3, of which 3 were waited for; matrix products, arithmetic and copies ran while one was open for 20% of the time, Pallas kernels for 0%

commit v1 on v0

v1 whole, which is shorter than its diff:
```python
import functools
import math

import jax
import jax.numpy as jnp
from jax import lax
from jax.experimental import pallas as pl
from jax.experimental.pallas import tpu as pltpu
from jax.sharding import PartitionSpec as P

HEAD = 128
PAIR = 2 * HEAD
BLOCK = 512
F32, BF16 = jnp.float32, jnp.bfloat16
VMEM_LIMIT = 56 * 1024 * 1024


def dot(a, b, contract):
    return lax.dot_general(a, b, (((contract[0],), (contract[1],)), ((), ())), preferred_element_type=F32)


def pair_states(left, right):
    both = dot(left, right, (0, 0))
    return both[:HEAD, :HEAD], both[HEAD:, HEAD:]


def as_rows(state, rows):
    return state.astype(BF16).reshape(HEAD // rows, rows, HEAD)


def first_kernel(mine_ref, grad_ref, weight_ref, key_ref, value_ref, part_ref, state_ref):
    del mine_ref
    rows = state_ref.shape[1]
    part_ref[...] = dot(grad_ref[...], weight_ref[...], (1, 1))
    one, two = pair_states(key_ref[...], value_ref[...])
    state_ref[: HEAD // rows] = as_rows(one, rows)
    state_ref[HEAD // rows :] = as_rows(two, rows)


def second_kernel(mine_ref, grad_ref, weight_ref, part_ref, query_ref, state_ref, head_ref, sent_ref):
    del mine_ref
    rows = state_ref.shape[1]
    head_grad = (part_ref[...] + dot(grad_ref[...], weight_ref[...], (1, 1))).astype(BF16)
    head_ref[...] = head_grad
    one, two = pair_states(query_ref[...], head_grad)
    sent_ref[:, 0] = state_ref[...]
    sent_ref[: HEAD // rows, 1] = as_rows(one, rows)
    sent_ref[HEAD // rows :, 1] = as_rows(two, rows)


def inner_kernel(factor, query_ref, key_ref, value_ref, head_ref, dq_ref, dk_ref, dv_ref):
    length = query_ref.shape[0]
    blocks = length // BLOCK
    later = lax.broadcasted_iota(jnp.int32, (BLOCK, BLOCK), 0)
    earlier = lax.broadcasted_iota(jnp.int32, (BLOCK, BLOCK), 1)
    causal = earlier <= later
    keys = jnp.zeros((HEAD, HEAD), F32)
    for b in range(blocks):
        at = pl.ds(b * BLOCK, BLOCK)
        q, k, v, g = query_ref[at, :], key_ref[at, :], value_ref[at, :], head_ref[at, :]
        probs = jnp.where(causal, factor * dot(q, k, (1, 1)), 0.0).astype(BF16)
        weight = jnp.where(causal, factor * dot(g, v, (1, 1)), 0.0).astype(BF16)
        dq = dot(weight, k, (1, 0))
        if b > 0:
            dq = dq + dot(g, (factor * keys).astype(BF16), (1, 1))
        dq_ref[at, :] = dq.astype(dq_ref.dtype)
        dk_ref[at, :] = dot(weight, q, (0, 0)).astype(dk_ref.dtype)
        dv_ref[at, :] = dot(probs, g, (0, 0)).astype(dv_ref.dtype)
        if b < blocks - 1:
            keys = keys + dot(k, v, (0, 0))
    grads = jnp.zeros((HEAD, HEAD), F32)
    for b in reversed(range(blocks - 1)):
        after, at = pl.ds((b + 1) * BLOCK, BLOCK), pl.ds(b * BLOCK, BLOCK)
        grads = grads + dot(query_ref[after, :], head_ref[after, :], (0, 0))
        low = (factor * grads).astype(BF16)
        dk_ref[at, :] = (dk_ref[at, :] + dot(value_ref[at, :], low, (1, 1))).astype(dk_ref.dtype)
        dv_ref[at, :] = (dv_ref[at, :] + dot(key_ref[at, :], low, (1, 0))).astype(dv_ref.dtype)


def middle_kernel(factor, given_ref, carried_ref):
    count, _, rows, width = given_ref.shape
    total = jnp.zeros((rows, width), F32)
    for i in range(count):
        carried_ref[i, 0] = (factor * total).astype(BF16)
        total = total + given_ref[i, 0].astype(F32)
    total = jnp.zeros((rows, width), F32)
    for i in reversed(range(count)):
        carried_ref[i, 1] = (factor * total).astype(BF16)
        total = total + given_ref[i, 1].astype(F32)


def last_kernel(carried_ref, key_ref, value_ref, head_ref, dq_in, dk_in, dv_in, dq_ref, dk_ref, dv_ref):
    chunks = carried_ref.shape[0] // 2
    for h in range(2):
        here, cols = pl.ds(h * chunks, chunks), pl.ds(h * HEAD, HEAD)
        before = carried_ref[here, 0].reshape(HEAD, HEAD)
        after = carried_ref[here, 1].reshape(HEAD, HEAD)
        dq_ref[:, cols] = (dq_in[:, cols] + dot(head_ref[:, cols], before, (1, 1))).astype(BF16)
        dk_ref[:, cols] = (dk_in[:, cols] + dot(value_ref[:, cols], after, (1, 1))).astype(BF16)
        dv_ref[:, cols] = (dv_in[:, cols] + dot(key_ref[:, cols], after, (1, 0))).astype(BF16)


def per_device(query_rows, key_rows, value_rows, out_grad, out_weight):
    length, width = query_rows.shape
    count = lax.axis_size("ctx")
    pairs = width // PAIR
    factor = 1.0 / math.sqrt(HEAD * length * count)
    rows = width // count
    chunks = PAIR // rows
    params = pltpu.CompilerParams(vmem_limit_bytes=VMEM_LIMIT)

    other_grad = lax.ppermute(out_grad, "head", [(0, 1), (1, 0)])
    mine = lax.axis_index("head").astype(jnp.int32).reshape(1)

    whole = pl.BlockSpec((length, width), lambda j, m: (0, 0))
    column = pl.BlockSpec((length, PAIR), lambda j, m: (0, j))
    state = pl.BlockSpec((chunks, rows, HEAD), lambda j, m: (j, 0, 0))
    both = pl.BlockSpec((chunks, 2, rows, HEAD), lambda j, m: (j, 0, 0, 0))
    product = 2 * length * width * width
    part, key_state = pl.pallas_call(
        first_kernel,
        grid_spec=pltpu.PrefetchScalarGridSpec(
            num_scalar_prefetch=1,
            grid=(pairs,),
            in_specs=[whole, pl.BlockSpec((PAIR, width), lambda j, m: (j, m[0])), column, column],
            out_specs=[column, state],
        ),
        out_shape=[
            jax.ShapeDtypeStruct((length, width), F32),
            jax.ShapeDtypeStruct((count, rows, HEAD), BF16),
        ],
        compiler_params=params,
        cost_estimate=pl.CostEstimate(flops=product * 2, bytes_accessed=12 * length * width, transcendentals=0),
        name="own_part",
    )(mine, out_grad, out_weight, key_rows, value_rows)
    head_grad, sent = pl.pallas_call(
        second_kernel,
        grid_spec=pltpu.PrefetchScalarGridSpec(
            num_scalar_prefetch=1,
            grid=(pairs,),
            in_specs=[
                whole,
                pl.BlockSpec((PAIR, width), lambda j, m: (j, 1 - m[0])),
                column,
                column,
                state,
            ],
            out_specs=[column, both],
        ),
        out_shape=[
            jax.ShapeDtypeStruct((length, width), BF16),
            jax.ShapeDtypeStruct((count, 2, rows, HEAD), BF16),
        ],
        compiler_params=params,
        cost_estimate=pl.CostEstimate(flops=product * 2, bytes_accessed=12 * length * width, transcendentals=0),
        name="other_part",
    )(mine, other_grad, out_weight, part, query_rows, key_state)

    given = lax.all_to_all(sent, "ctx", 0, 0)

    head = pl.BlockSpec((length, HEAD), lambda h: (0, h))
    local = pl.pallas_call(
        functools.partial(inner_kernel, factor),
        grid=(width // HEAD,),
        in_specs=[head] * 4,
        out_specs=[head] * 3,
        out_shape=[jax.ShapeDtypeStruct((length, width), F32)] * 3,
        compiler_params=params,
        cost_estimate=pl.CostEstimate(flops=product * 4, bytes_accessed=20 * length * width, transcendentals=0),
        name="inner",
    )(query_rows, key_rows, value_rows, head_grad)

    carried = pl.pallas_call(
        functools.partial(middle_kernel, factor),
        out_shape=jax.ShapeDtypeStruct(given.shape, BF16),
        name="sums",
    )(given)
    carried = lax.all_to_all(carried, "ctx", 0, 0)

    column = pl.BlockSpec((length, PAIR), lambda j: (0, j))
    return pl.pallas_call(
        last_kernel,
        grid=(pairs,),
        in_specs=[pl.BlockSpec((chunks, 2, rows, HEAD), lambda j: (j, 0, 0, 0))] + [column] * 6,
        out_specs=[column] * 3,
        out_shape=[jax.ShapeDtypeStruct((length, width), BF16)] * 3,
        compiler_params=params,
        cost_estimate=pl.CostEstimate(flops=product, bytes_accessed=24 * length * width, transcendentals=0),
        name="carried_part",
    )(carried, key_rows, value_rows, head_grad, *local)


def solution(mesh):
    rows = P("ctx", "head")
    return jax.shard_map(
        per_device,
        mesh=mesh,
        in_specs=(rows, rows, rows, rows, P("head", None)),
        out_specs=(rows, rows, rows),
        check_vma=False,
    )
```

time: 551 us -> 79.5 us (0.14); the launches traced: 544 us -> 78.7 us
  waiting for transfers between devices: 239 us -> 0.01 us
  other arithmetic: 156 us -> 0 us
  local copies, waits for them, and re-layouts: 69.1 us -> 2.11 us
  matrix products: 62.4 us -> 0 us
  Pallas kernels: 0 us -> 45.8 us
  blocking collectives: 0 us -> 23.9 us
  between operations: 13.9 us -> 0.66 us
  starting transfers between devices: 0.12 us -> 6.19 us
    all_gather x3 -> x0, waiting for transfers between devices: 238 us -> none  [the longest x2 230 us: carried_in(): pieces = lax.all_gather(value, axis)]
    select_n x126 -> x0, other arithmetic: 156 us -> none  [step(): return jnp.where(position < mine, longer, subtotal)]
    dot_general x17 -> x0, matrix products: 62.4 us -> none  [the longest x2 9.86 us: one_block(): jnp.einsum('hts,thv->shv', probs_low, gradient_segment, preferred_element...]
    pallas_call x0 -> x5, Pallas kernels: none -> 45.8 us  [the longest x1 17.9 us: per_device(): pl.pallas_call(functools.partial(inner_kernel, factor), grid=(width // HE...]
    all_to_all x0 -> x1, blocking collectives: none -> 23.9 us  [per_device(): given = lax.all_to_all(sent, 'ctx', 0, 0)]
    rev x1 -> x0, local copies, waits for them, and re-layouts: 23 us -> none  [carried_in(): pieces = pieces[::-1]]
    dynamic_update_slice x10 -> x0, local copies, waits for them, and re-layouts: 13.4 us -> none  [per_device(): lax.scan(one_block, start_carry, (qblock, kblock, vblock, gblock, key_sta...]
    unnamed x17 -> x4, local copies, waits for them, and re-layouts: 13.6 us -> 2.11 us
  transfers between devices with their start and end apart: 3 -> 2, of which waited for: 3 -> 0; matrix products, arithmetic and copies ran while one was open for 20% -> 0% of each run, Pallas kernels for 0% -> 33%
where the time goes in v1:
time: 79.5 us; the launch traced here: 78.7 us
  Pallas kernels  45.8 us (58%)
  blocking collectives  23.9 us (30%)
  starting transfers between devices  6.19 us (8%)
  local copies, waits for them, and re-layouts  2.11 us (3%)
    all_to_all x1, blocking collectives, per_device(): given = lax.all_to_all(sent, 'ctx', 0, 0)  23.9 us
    pallas_call x1, Pallas kernels, per_device(): pl.pallas_call(functools.partial(inner_kernel, factor), grid=(width // HE...  17.9 us
    pallas_call x1, Pallas kernels, per_device(): pl.pallas_call(last_kernel, grid=(pairs,), in_specs=[pl.BlockSpec((chunks...  9.73 us
    pallas_call x1, Pallas kernels, per_device(): pl.pallas_call(second_kernel, grid_spec=pltpu.PrefetchScalarGridSpec(num_...  8.22 us
    pallas_call x1, Pallas kernels, per_device(): pl.pallas_call(first_kernel, grid_spec=pltpu.PrefetchScalarGridSpec(num_s...  7.93 us
    all_to_all x1, starting transfers between devices, per_device(): carried = lax.all_to_all(carried, 'ctx', 0, 0)  4.69 us
    unnamed x4, local copies, waits for them, and re-layouts  2.11 us
    pallas_call x1, Pallas kernels, per_device(): pl.pallas_call(functools.partial(middle_kernel, factor), out_shape=jax.Sh...  1.96 us
  transfers between devices with their start and end apart: 2, of which 0 were waited for; matrix products, arithmetic and copies ran while one was open for 0% of the time, Pallas kernels for 33%

profile of v1, /device:TPU:1, one launch (start us, length us, event | category | flops | bytes accessed | tf_op | source)
XLA Modules:
  0.0 78.7 jit_solution(14410955060782680938)
XLA Ops:
  0.6 1.5 %collective-permute-start = (bf16[1024,1024]{1,0:T(8,128)(2,1)}, bf16[1024,1024]{1,0:T(8,128)(2,1)S(1)}, u32[]{:S(2)}, u32[]{:S(2)}) collective-permute-start(bf16[1024,1024]{1,0:T(8,128)(2,1)} %grad_ref.1), channel_id=1, source_target_pairs={{0,1},{1,0},{2,3},{3,2},{4,5},{5,4},{6,7},{7,6},{8,9},{9,8},{10,11... | collective-permute-start | bytes 6291464 | tf_op jit(solution)/shard_map/ppermute | solution.py:112
  2.1 7.9 %own_part.1 = (f32[1024,1024]{1,0:T(8,128)}, bf16[64,16,128]{2,1,0:T(8,128)(2,1)}) custom-call(s32[1]{0:T(128)} %bitcast.mine_ref, bf16[1024,1024]{1,0:T(8,128)(2,1)} %grad_ref.1, bf16[1024,2048]{1,0:T(8,128)(2,1)} %weight_ref.3, bf16[1024,1024]{1,0:T(8,128)(2,1)} %key_ref.5, bf16[1024,1024]{1,0:T(8,128)(2,1)} %value_ref.5), custom_call_target="tpu_custom_call" | custom-call | flops 4294967296 | bytes 12582912 | tf_op jit(solution)/shard_map/own_part/pallas_call | solution.py:120
  10.1 0.0 collective-permute-done.grad_ref
  10.1 0.0 copy-start.1
  10.1 1.3 %copy-done.1 = bf16[1024,1024]{1,0:T(8,128)(2,1)} copy-done((bf16[1024,1024]{1,0:T(8,128)(2,1)}, bf16[1024,1024]{1,0:T(8,128)(2,1)S(1)}, u32[]{:S(2)}) %copy-start.1) | copy-done | bytes 2097176
  11.4 8.2 %other_part.1 = (bf16[1024,1024]{1,0:T(8,128)(2,1)}, bf16[64,2,16,128]{3,2,1,0:T(8,128)(2,1)}) custom-call(s32[1]{0:T(128)} %bitcast.mine_ref, bf16[1024,1024]{1,0:T(8,128)(2,1)} %copy-done.1, bf16[1024,2048]{1,0:T(8,128)(2,1)} %weight_ref.3, f32[1024,1024]{1,0:T(8,128)} %get-tuple-element.10.part_ref, bf16[1024,1024]{1,0:T(8,128)(2,1)} %query_ref.3, ...), custom_call_target="tpu_custom_call" | custom-call | flops 4294967296 | bytes 12582912 | tf_op jit(solution)/shard_map/other_part/pallas_call | solution.py:136
  19.6 23.9 %all_to_all.10.given_ref = bf16[64,2,16,128]{3,2,1,0:T(8,128)(2,1)} all-to-all(bf16[64,2,16,128]{3,2,1,0:T(8,128)(2,1)} %get-tuple-element.12), channel_id=1, replica_groups=mesh['ctx'=64,'head'=2] {'ctx'}, dimensions={0} | all-to-all | bytes 1048576 | tf_op jit(solution)/shard_map/all_to_all | solution.py:159
  43.6 2.0 %sums.1 = bf16[64,2,16,128]{3,2,1,0:T(8,128)(2,1)} custom-call(bf16[64,2,16,128]{3,2,1,0:T(8,128)(2,1)} %all_to_all.10.given_ref), custom_call_target="tpu_custom_call" | custom-call | tf_op jit(solution)/shard_map/sums/pallas_call | solution.py:173
  45.5 4.7 %all-to-all-start.1 = ((bf16[64,2,16,128]{3,2,1,0:T(8,128)(2,1)}), bf16[64,2,16,128]{3,2,1,0:T(8,128)(2,1)S(1)}, u32[]{:S(2)}, u32[]{:S(2)}) async-start(bf16[64,2,16,128]{3,2,1,0:T(8,128)(2,1)} %sums.1), calls=%async_computation.1 | async-start | bytes 1048576 | tf_op jit(solution)/shard_map/all_to_all | solution.py:178
  50.2 17.9 %inner.1 = (f32[1024,1024]{1,0:T(8,128)}, f32[1024,1024]{1,0:T(8,128)}, f32[1024,1024]{1,0:T(8,128)}) custom-call(bf16[1024,1024]{1,0:T(8,128)(2,1)} %query_ref.3, bf16[1024,1024]{1,0:T(8,128)(2,1)} %key_ref.5, bf16[1024,1024]{1,0:T(8,128)(2,1)} %value_ref.5, bf16[1024,1024]{1,0:T(8,128)(2,1)} %get-tuple-element.13.head_ref), custom_call_target="tpu_custom_call" | custom-call | flops 8589934592 | bytes 20971520 | tf_op jit(solution)/shard_map/inner/pallas_call | solution.py:162
  68.2 0.0 all-to-all-done.1.carried_ref
  68.2 0.0 copy-start
  68.2 0.8 %copy-done = bf16[64,2,16,128]{3,2,1,0:T(8,128)(2,1)} copy-done((bf16[64,2,16,128]{3,2,1,0:T(8,128)(2,1)}, bf16[64,2,16,128]{3,2,1,0:T(8,128)(2,1)S(1)}, u32[]{:S(2)}) %copy-start) | copy-done | bytes 524312
  69.0 9.7 %carried_part.1 = (bf16[1024,1024]{1,0:T(8,128)(2,1)}, bf16[1024,1024]{1,0:T(8,128)(2,1)}, bf16[1024,1024]{1,0:T(8,128)(2,1)}) custom-call(bf16[64,2,16,128]{3,2,1,0:T(8,128)(2,1)} %copy-done, bf16[1024,1024]{1,0:T(8,128)(2,1)} %key_ref.5, bf16[1024,1024]{1,0:T(8,128)(2,1)} %value_ref.5, bf16[1024,1024]{1,0:T(8,128)(2,1)} %get-tuple-element.13.head_ref, ...), custom_call_target="tpu_custom_call" | custom-call | flops 2147483648 | bytes 25165824 | tf_op jit(solution)/shard_map/carried_part/pallas_call | solution.py:181
Async XLA Ops:
  0.6 9.4 %collective-permute-start = (bf16[1024,1024]{1,0:T(8,128)(2,1)}, bf16[1024,1024]{1,0:T(8,128)(2,1)S(1)}, u32[]{:S(2)}, u32[]{:S(2)}) collective-permute-start(bf16[1024,1024]{1,0:T(8,128)(2,1)} %grad_ref.1), channel_id=1, source_target_pairs={{0,1},{1,0},{2,3},{3,2},{4,5},{5,4},{6,7},{7,6},{8,9},{9,8},{10,11... | collective-permute-start | bytes 6291464 | tf_op jit(solution)/shard_map/ppermute | solution.py:112
  10.1 1.3 %copy-start.1 = (bf16[1024,1024]{1,0:T(8,128)(2,1)}, bf16[1024,1024]{1,0:T(8,128)(2,1)S(1)}, u32[]{:S(2)}) copy-start(bf16[1024,1024]{1,0:T(8,128)(2,1)S(1)} %collective-permute-done.grad_ref) | copy-start | bytes 6291460
  45.5 22.6 %all-to-all-start.1 = ((bf16[64,2,16,128]{3,2,1,0:T(8,128)(2,1)}), bf16[64,2,16,128]{3,2,1,0:T(8,128)(2,1)S(1)}, u32[]{:S(2)}, u32[]{:S(2)}) async-start(bf16[64,2,16,128]{3,2,1,0:T(8,128)(2,1)} %sums.1), calls=%async_computation.1 | async-start | bytes 1048576 | tf_op jit(solution)/shard_map/all_to_all | solution.py:178
  68.2 0.8 %copy-start = (bf16[64,2,16,128]{3,2,1,0:T(8,128)(2,1)}, bf16[64,2,16,128]{3,2,1,0:T(8,128)(2,1)S(1)}, u32[]{:S(2)}) copy-start(bf16[64,2,16,128]{3,2,1,0:T(8,128)(2,1)S(1)} %all-to-all-done.1.carried_ref) | copy-start | bytes 1572868

commit v2 on v1

v2 whole, which is shorter than its diff:
```python
import functools
import math

import jax
import jax.numpy as jnp
from jax import lax
from jax.experimental import pallas as pl
from jax.experimental.pallas import tpu as pltpu
from jax.sharding import PartitionSpec as P

HEAD = 128
PAIR = 2 * HEAD
BLOCK = 512
TILE = 256
F32, BF16 = jnp.float32, jnp.bfloat16
MIB = 1024 * 1024
IN_VMEM = pl.BlockSpec(memory_space=pltpu.VMEM)
ANYWHERE = pl.BlockSpec(memory_space=pl.ANY)


def near(*arrays):
    return [pltpu.with_memory_space_constraint(a, pltpu.VMEM) for a in arrays]


def far(*arrays):
    return [pltpu.with_memory_space_constraint(a, pltpu.HBM) for a in arrays]


def dot(a, b, contract):
    return lax.dot_general(a, b, (((contract[0],), (contract[1],)), ((), ())), preferred_element_type=F32)


def columns(j, size):
    return pl.ds(pl.multiple_of(j * size, size), size)


def of_head(h):
    return slice(h * HEAD, (h + 1) * HEAD)


def pair_states(left, right):
    both = dot(left, right, (0, 0))
    return both[:HEAD, :HEAD], both[HEAD:, HEAD:]


def as_rows(state, rows):
    return state.astype(BF16).reshape(HEAD // rows, rows, HEAD)


def first_kernel(mine_ref, grad_ref, weight_ref, key_ref, value_ref, part_ref, state_ref):
    del mine_ref
    rows = state_ref.shape[1]
    one, two = pair_states(key_ref[...], value_ref[...])
    state_ref[: HEAD // rows] = as_rows(one, rows)
    state_ref[HEAD // rows :] = as_rows(two, rows)
    part_ref[:, columns(pl.program_id(0), PAIR)] = dot(grad_ref[...], weight_ref[...], (1, 1))


def second_kernel(mine_ref, grad_ref, weight_ref, part_ref, query_ref, state_ref, head_ref, sent_ref, sum_ref):
    i = pl.program_id(0)
    width = grad_ref.shape[1]
    here = columns(i, TILE)
    other = dot(grad_ref[...], weight_ref[:, columns(1 - mine_ref[0], width)], (1, 1))
    head_ref[...] = (part_ref[here, :] + other).astype(BF16)

    @pl.when(i == 0)
    def _():
        sum_ref[...] = jnp.zeros_like(sum_ref)

    for h in range(width // HEAD):
        sum_ref[of_head(h), :] += dot(query_ref[here, of_head(h)], head_ref[:, of_head(h)], (0, 0))

    @pl.when(i == pl.num_programs(0) - 1)
    def _():
        sent_ref[:, 0] = state_ref[...]
        sent_ref[:, 1] = sum_ref[...].astype(BF16).reshape(state_ref.shape)


def inner_kernel(factor, after_ref, query_ref, key_ref, value_ref, head_ref, dq_ref, dk_ref, dv_ref):
    del after_ref
    blocks = query_ref.shape[0] // BLOCK
    later = lax.broadcasted_iota(jnp.int32, (BLOCK, BLOCK), 0)
    earlier = lax.broadcasted_iota(jnp.int32, (BLOCK, BLOCK), 1)
    causal = earlier <= later
    spans = [pl.ds(b * BLOCK, BLOCK) for b in range(blocks)]
    before, after = [None] * blocks, [None] * blocks
    for b in range(1, blocks):
        state = dot(key_ref[spans[b - 1], :], value_ref[spans[b - 1], :], (0, 0))
        before[b] = state if b == 1 else before[b - 1] + state
    for b in reversed(range(blocks - 1)):
        state = dot(query_ref[spans[b + 1], :], head_ref[spans[b + 1], :], (0, 0))
        after[b] = state if b == blocks - 2 else after[b + 1] + state
    for b, at in enumerate(spans):
        q, k, v, g = query_ref[at, :], key_ref[at, :], value_ref[at, :], head_ref[at, :]
        probs = jnp.where(causal, factor * dot(q, k, (1, 1)), 0.0).astype(BF16)
        weight = jnp.where(causal, factor * dot(g, v, (1, 1)), 0.0).astype(BF16)
        dq, dk, dv = dot(weight, k, (1, 0)), dot(weight, q, (0, 0)), dot(probs, g, (0, 0))
        if before[b] is not None:
            dq = dq + dot(g, (factor * before[b]).astype(BF16), (1, 1))
        if after[b] is not None:
            low = (factor * after[b]).astype(BF16)
            dk = dk + dot(v, low, (1, 1))
            dv = dv + dot(k, low, (1, 0))
        dq_ref[at, :], dk_ref[at, :], dv_ref[at, :] = dq.astype(BF16), dk.astype(BF16), dv.astype(BF16)


def middle_kernel(factor, given_ref, after_ref, carried_ref):
    del after_ref
    count, _, rows, width = given_ref.shape
    total = jnp.zeros((rows, width), F32)
    for i in range(count):
        carried_ref[i, 0] = (factor * total).astype(BF16)
        total = total + given_ref[i, 0].astype(F32)
    total = jnp.zeros((rows, width), F32)
    for i in reversed(range(count)):
        carried_ref[i, 1] = (factor * total).astype(BF16)
        total = total + given_ref[i, 1].astype(F32)


def last_kernel(carried_ref, key_ref, value_ref, head_ref, *refs):
    halves, (dq_ref, dk_ref, dv_ref) = (refs[:3], refs[3:6]), refs[6:]
    each = HEAD // carried_ref.shape[2]
    heads = key_ref.shape[1] // HEAD
    for h in range(heads):
        dq_in, dk_in, dv_in = halves[2 * h // heads]
        col, at = of_head(h), slice(h * each, (h + 1) * each)
        low = of_head(h % (heads // 2))
        before = carried_ref[at, 0].reshape(HEAD, HEAD)
        after = carried_ref[at, 1].reshape(HEAD, HEAD)
        dq_ref[:, col] = (dq_in[:, low] + dot(head_ref[:, col], before, (1, 1))).astype(BF16)
        dk_ref[:, col] = (dk_in[:, low] + dot(value_ref[:, col], after, (1, 1))).astype(BF16)
        dv_ref[:, col] = (dv_in[:, low] + dot(key_ref[:, col], after, (1, 0))).astype(BF16)


def per_device(query_rows, key_rows, value_rows, out_grad, out_weight):
    length, width = query_rows.shape
    count = lax.axis_size("ctx")
    pairs, heads = width // PAIR, width // HEAD
    factor = 1.0 / math.sqrt(HEAD * length * count)
    rows = width // count
    params = pltpu.CompilerParams(vmem_limit_bytes=16 * MIB)
    product = 2 * length * width * width
    area = length * width

    def cost(flops, bytes_accessed):
        return pl.CostEstimate(flops=int(flops), bytes_accessed=int(bytes_accessed), transcendentals=0)

    other_grad = lax.ppermute(out_grad, "head", [(0, 1), (1, 0)])
    mine = lax.axis_index("head").astype(jnp.int32).reshape(1)

    column = pl.BlockSpec((length, PAIR), lambda j, m: (0, j))
    part, key_state = pl.pallas_call(
        first_kernel,
        grid_spec=pltpu.PrefetchScalarGridSpec(
            num_scalar_prefetch=1,
            grid=(pairs,),
            in_specs=[
                pl.BlockSpec((length, width), lambda j, m: (0, 0)),
                pl.BlockSpec((PAIR, width), lambda j, m: (j, m[0])),
                column,
                column,
            ],
            out_specs=[IN_VMEM, pl.BlockSpec((PAIR // rows, rows, HEAD), lambda j, m: (j, 0, 0))],
        ),
        out_shape=[pltpu.VMEM((length, width), F32), jax.ShapeDtypeStruct((count, rows, HEAD), BF16)],
        compiler_params=params,
        cost_estimate=cost(2 * product, 8 * area),
        name="own_part",
    )(mine, *far(out_grad, out_weight, key_rows, value_rows))

    tile = pl.BlockSpec((TILE, width), lambda i, m: (i, 0))
    head_grad, sent = pl.pallas_call(
        second_kernel,
        grid_spec=pltpu.PrefetchScalarGridSpec(
            num_scalar_prefetch=1,
            grid=(length // TILE,),
            in_specs=[tile, IN_VMEM, IN_VMEM, IN_VMEM, IN_VMEM],
            out_specs=[tile, IN_VMEM],
            scratch_shapes=[pltpu.VMEM((width, HEAD), F32)],
        ),
        out_shape=[pltpu.HBM((length, width), BF16), pltpu.VMEM((count, 2, rows, HEAD), BF16)],
        compiler_params=params,
        cost_estimate=cost(2 * product, 8 * area),
        name="other_part",
    )(mine, *far(other_grad), *near(out_weight, part, query_rows, key_state))

    given = lax.all_to_all(sent, "ctx", 0, 0)

    def inner(base, number, after):
        return pl.pallas_call(
            functools.partial(inner_kernel, factor),
            grid=(number,),
            in_specs=[ANYWHERE] + [pl.BlockSpec((length, HEAD), lambda h: (0, h + base))] * 4,
            out_specs=[pl.BlockSpec((length, HEAD), lambda h: (0, h))] * 3,
            out_shape=[pltpu.HBM((length, number * HEAD), BF16)] * 3,
            compiler_params=params,
            cost_estimate=cost(6 * product * number / heads, 10 * area),
            name=f"inner_{base}",
        )(after, *far(query_rows, key_rows, value_rows, head_grad))

    half = heads // 2
    local_a = inner(0, half, key_state)
    carried = pl.pallas_call(
        functools.partial(middle_kernel, factor),
        in_specs=[IN_VMEM, ANYWHERE],
        out_specs=IN_VMEM,
        out_shape=pltpu.VMEM(given.shape, BF16),
        compiler_params=pltpu.CompilerParams(vmem_limit_bytes=4 * MIB),
        name="sums",
    )(*near(given), *far(local_a[0]))
    local_b = inner(half, heads - half, carried)
    carried = lax.all_to_all(carried, "ctx", 0, 0)

    tile = pl.BlockSpec((TILE, width), lambda i: (i, 0))
    return pl.pallas_call(
        last_kernel,
        grid=(length // TILE,),
        in_specs=[IN_VMEM] + [tile] * 3 + [pl.BlockSpec((TILE, width // 2), lambda i: (i, 0))] * 6,
        out_specs=[tile] * 3,
        out_shape=[jax.ShapeDtypeStruct((length, width), BF16)] * 3,
        compiler_params=params,
        cost_estimate=cost(product, 18 * area),
        name="carried_part",
    )(*near(carried), *far(key_rows, value_rows, head_grad, *local_a, *local_b))


def solution(mesh):
    rows = P("ctx", "head")
    return jax.shard_map(
        per_device,
        mesh=mesh,
        in_specs=(rows, rows, rows, rows, P("head", None)),
        out_specs=(rows, rows, rows),
        check_vma=False,
    )
```

time: 79.5 us -> 68.3 us (0.86)
  blocking collectives: 23.9 us -> 0 us
  starting transfers between devices: 6.19 us -> 19.2 us
  waiting for transfers between devices: 0.01 us -> 6.03 us
  Pallas kernels: 45.8 us -> 41.2 us
  local copies, waits for them, and re-layouts: 2.11 us -> 0.01 us
    all_to_all x1 -> x0, blocking collectives: 23.9 us -> none  [per_device(): given = lax.all_to_all(sent, 'ctx', 0, 0)]
    all_to_all x0 -> x1, starting transfers between devices: none -> 11.2 us  [per_device(): given = lax.all_to_all(sent, 'ctx', 0, 0)]
    all_to_all x0 -> x1, waiting for transfers between devices: none -> 3.33 us  [per_device(): given = lax.all_to_all(sent, 'ctx', 0, 0)]
    all_to_all x1, waiting for transfers between devices: 0.01 us -> 2.7 us  [per_device(): carried = lax.all_to_all(carried, 'ctx', 0, 0)]
    unnamed x4, local copies, waits for them, and re-layouts: 2.11 us -> 0.01 us
    pallas_call x3 -> x4, Pallas kernels: 29.6 us -> 27.8 us  [the longest x2 18.7 us: inner(): pl.pallas_call(functools.partial(inner_kernel, factor), grid=(number,), i...]
    all_to_all x1, starting transfers between devices: 4.69 us -> 6.45 us  [per_device(): carried = lax.all_to_all(carried, 'ctx', 0, 0)]
    pallas_call x1, Pallas kernels: 8.22 us -> 6.7 us  [per_device(): pl.pallas_call(second_kernel, grid_spec=pltpu.PrefetchScalarGridSpec(num_...]
  transfers between devices with their start and end apart: 2 -> 3, of which waited for: 0 -> 2; matrix products, arithmetic and copies ran while one was open for 0% -> 0% of each run, Pallas kernels for 33% -> 38%
where the time goes in v2:
time: 68.3 us; the launch traced here: 67.1 us
  Pallas kernels  41.2 us (60%)
  starting transfers between devices  19.2 us (28%)
  waiting for transfers between devices  6.03 us (9%)
    pallas_call x2, Pallas kernels, inner(): pl.pallas_call(functools.partial(inner_kernel, factor), grid=(number,), i...  18.7 us
    all_to_all x1, starting transfers between devices, per_device(): given = lax.all_to_all(sent, 'ctx', 0, 0)  11.2 us
    pallas_call x1, Pallas kernels, per_device(): pl.pallas_call(last_kernel, grid=(length // TILE,), in_specs=[IN_VMEM] +...  8.21 us
    pallas_call x1, Pallas kernels, per_device(): pl.pallas_call(second_kernel, grid_spec=pltpu.PrefetchScalarGridSpec(num_...  6.7 us
    pallas_call x1, Pallas kernels, per_device(): pl.pallas_call(first_kernel, grid_spec=pltpu.PrefetchScalarGridSpec(num_s...  6.67 us
    all_to_all x1, starting transfers between devices, per_device(): carried = lax.all_to_all(carried, 'ctx', 0, 0)  6.45 us
    all_to_all x1, waiting for transfers between devices, per_device(): given = lax.all_to_all(sent, 'ctx', 0, 0)  3.33 us
    all_to_all x1, waiting for transfers between devices, per_device(): carried = lax.all_to_all(carried, 'ctx', 0, 0)  2.7 us
  transfers between devices with their start and end apart: 3, of which 2 were waited for; matrix products, arithmetic and copies ran while one was open for 0% of the time, Pallas kernels for 38%

profile of v2, /device:TPU:1, one launch (start us, length us, event | category | flops | bytes accessed | tf_op | source)
XLA Modules:
  0.0 67.1 jit_solution(14252767836658077222)
XLA Ops:
  0.6 1.5 %collective-permute-start = (bf16[1024,1024]{1,0:T(8,128)(2,1)}, bf16[1024,1024]{1,0:T(8,128)(2,1)}, u32[]{:S(2)}, u32[]{:S(2)}) collective-permute-start(bf16[1024,1024]{1,0:T(8,128)(2,1)} %grad_ref.1), channel_id=1, source_target_pairs={{0,1},{1,0},{2,3},{3,2},{4,5},{5,4},{6,7},{7,6},{8,9},{9,8},{10,11... | collective-permute-start | bytes 6291464 | tf_op jit(solution)/shard_map/ppermute | solution.py:148
  2.1 0.0 copy-start
  2.1 0.0 copy-start.1
  2.1 6.7 %own_part.1 = (f32[1024,1024]{1,0:T(8,128)S(1)}, bf16[64,16,128]{2,1,0:T(8,128)(2,1)S(1)}) custom-call(s32[1]{0:T(128)} %bitcast.mine_ref, bf16[1024,1024]{1,0:T(8,128)(2,1)} %grad_ref.1, bf16[1024,2048]{1,0:T(8,128)(2,1)} %weight_ref.3, bf16[1024,1024]{1,0:T(8,128)(2,1)} %key_ref.7, bf16[1024,1024]{1,0:T(8,128)(2,1)} %value_ref.7), custom_call_target="tpu_custom_call" | custom-call | flops 4294967296 | bytes 8388608 | tf_op jit(solution)/shard_map/own_part/pallas_call | solution.py:152
  8.8 0.0 collective-permute-done.grad_ref
  8.8 0.0 copy-done
  8.8 0.0 copy-done.1
  8.8 6.7 %other_part.1 = (bf16[1024,1024]{1,0:T(8,128)(2,1)}, bf16[64,2,16,128]{3,2,1,0:T(8,128)(2,1)}) custom-call(s32[1]{0:T(128)} %bitcast.mine_ref, bf16[1024,1024]{1,0:T(8,128)(2,1)} %collective-permute-done.grad_ref, bf16[1024,2048]{1,0:T(8,128)(2,1)S(1)} %copy-done, f32[1024,1024]{1,0:T(8,128)S(1)} %get-tuple-element.13.part_ref, ...), custom_call_target="tpu_custom_call" | custom-call | flops 4294967296 | bytes 8388608 | tf_op jit(solution)/shard_map/other_part/pallas_call | solution.py:172
  15.5 11.2 %all-to-all-start = ((bf16[64,2,16,128]{3,2,1,0:T(8,128)(2,1)}), bf16[64,2,16,128]{3,2,1,0:T(8,128)(2,1)S(1)}, u32[]{:S(2)}, u32[]{:S(2)}) async-start(bf16[64,2,16,128]{3,2,1,0:T(8,128)(2,1)} %get-tuple-element.15), calls=%async_computation | async-start | bytes 1048576 | tf_op jit(solution)/shard_map/all_to_all | solution.py:187
  26.8 9.3 %inner_0.1 = (bf16[1024,512]{1,0:T(8,128)(2,1)}, bf16[1024,512]{1,0:T(8,128)(2,1)}, bf16[1024,512]{1,0:T(8,128)(2,1)}) custom-call(bf16[64,16,128]{2,1,0:T(8,128)(2,1)S(1)} %get-tuple-element.14.state_ref.after_ref, bf16[1024,1024]{1,0:T(8,128)(2,1)} %query_ref.5, bf16[1024,1024]{1,0:T(8,128)(2,1)} %key_ref.7, bf16[1024,1024]{1,0:T(8,128)(2,1)} %value_ref.7, ...), custom_call_target="tpu_custom_call" | custom-call | flops 6442450944 | bytes 10485760 | tf_op jit(solution)/shard_map/inner_0/pallas_call | solution.py:190
  36.1 3.3 %all-to-all-done.given_ref = bf16[64,2,16,128]{3,2,1,0:T(8,128)(2,1)S(1)} async-done(((bf16[64,2,16,128]{3,2,1,0:T(8,128)(2,1)}), bf16[64,2,16,128]{3,2,1,0:T(8,128)(2,1)S(1)}, u32[]{:S(2)}, u32[]{:S(2)}) %all-to-all-start) | async-done | bytes 524320 | tf_op jit(solution)/shard_map/all_to_all | solution.py:187
  39.4 0.9 %sums.1.after_ref = bf16[64,2,16,128]{3,2,1,0:T(8,128)(2,1)} custom-call(bf16[64,2,16,128]{3,2,1,0:T(8,128)(2,1)S(1)} %all-to-all-done.given_ref, bf16[1024,512]{1,0:T(8,128)(2,1)} %get-tuple-element.17.after_ref.refs_0_), custom_call_target="tpu_custom_call" | custom-call | tf_op jit(solution)/shard_map/sums/pallas_call | solution.py:203
  40.4 6.4 %all-to-all-start.1 = ((bf16[64,2,16,128]{3,2,1,0:T(8,128)(2,1)}), bf16[64,2,16,128]{3,2,1,0:T(8,128)(2,1)S(1)}, u32[]{:S(2)}, u32[]{:S(2)}) async-start(bf16[64,2,16,128]{3,2,1,0:T(8,128)(2,1)} %sums.1.after_ref), calls=%async_computation.1 | async-start | bytes 1048576 | tf_op jit(solution)/shard_map/all_to_all | solution.py:212
  46.8 9.3 %inner_4.1 = (bf16[1024,512]{1,0:T(8,128)(2,1)}, bf16[1024,512]{1,0:T(8,128)(2,1)}, bf16[1024,512]{1,0:T(8,128)(2,1)}) custom-call(bf16[64,2,16,128]{3,2,1,0:T(8,128)(2,1)} %sums.1.after_ref, bf16[1024,1024]{1,0:T(8,128)(2,1)} %query_ref.5, bf16[1024,1024]{1,0:T(8,128)(2,1)} %key_ref.7, bf16[1024,1024]{1,0:T(8,128)(2,1)} %value_ref.7, ...), custom_call_target="tpu_custom_call" | custom-call | flops 6442450944 | bytes 10485760 | tf_op jit(solution)/shard_map/inner_4/pallas_call | solution.py:190
  56.2 2.7 %all-to-all-done.1.carried_ref = bf16[64,2,16,128]{3,2,1,0:T(8,128)(2,1)S(1)} async-done(((bf16[64,2,16,128]{3,2,1,0:T(8,128)(2,1)}), bf16[64,2,16,128]{3,2,1,0:T(8,128)(2,1)S(1)}, u32[]{:S(2)}, u32[]{:S(2)}) %all-to-all-start.1) | async-done | bytes 524320 | tf_op jit(solution)/shard_map/all_to_all | solution.py:212
  58.9 8.2 %carried_part.1 = (bf16[1024,1024]{1,0:T(8,128)(2,1)}, bf16[1024,1024]{1,0:T(8,128)(2,1)}, bf16[1024,1024]{1,0:T(8,128)(2,1)}) custom-call(bf16[64,2,16,128]{3,2,1,0:T(8,128)(2,1)S(1)} %all-to-all-done.1.carried_ref, bf16[1024,1024]{1,0:T(8,128)(2,1)} %key_ref.7, bf16[1024,1024]{1,0:T(8,128)(2,1)} %value_ref.7, ...), custom_call_target="tpu_custom_call" | custom-call | flops 2147483648 | bytes 18874368 | tf_op jit(solution)/shard_map/carried_part/pallas_call | solution.py:215
Async XLA Ops:
  0.6 8.2 %collective-permute-start = (bf16[1024,1024]{1,0:T(8,128)(2,1)}, bf16[1024,1024]{1,0:T(8,128)(2,1)}, u32[]{:S(2)}, u32[]{:S(2)}) collective-permute-start(bf16[1024,1024]{1,0:T(8,128)(2,1)} %grad_ref.1), channel_id=1, source_target_pairs={{0,1},{1,0},{2,3},{3,2},{4,5},{5,4},{6,7},{7,6},{8,9},{9,8},{10,11... | collective-permute-start | bytes 6291464 | tf_op jit(solution)/shard_map/ppermute | solution.py:148
  2.1 6.7 %copy-start = (bf16[1024,2048]{1,0:T(8,128)(2,1)S(1)}, bf16[1024,2048]{1,0:T(8,128)(2,1)}, u32[]{:S(2)}) copy-start(bf16[1024,2048]{1,0:T(8,128)(2,1)} %weight_ref.3) | copy-start | bytes 12582916
  2.1 6.7 %copy-start.1 = (bf16[1024,1024]{1,0:T(8,128)(2,1)S(1)}, bf16[1024,1024]{1,0:T(8,128)(2,1)}, u32[]{:S(2)}) copy-start(bf16[1024,1024]{1,0:T(8,128)(2,1)} %query_ref.5) | copy-start | bytes 6291460
  15.5 23.9 %all-to-all-start = ((bf16[64,2,16,128]{3,2,1,0:T(8,128)(2,1)}), bf16[64,2,16,128]{3,2,1,0:T(8,128)(2,1)S(1)}, u32[]{:S(2)}, u32[]{:S(2)}) async-start(bf16[64,2,16,128]{3,2,1,0:T(8,128)(2,1)} %get-tuple-element.15), calls=%async_computation | async-start | bytes 1048576 | tf_op jit(solution)/shard_map/all_to_all | solution.py:187
  40.4 18.5 %all-to-all-start.1 = ((bf16[64,2,16,128]{3,2,1,0:T(8,128)(2,1)}), bf16[64,2,16,128]{3,2,1,0:T(8,128)(2,1)S(1)}, u32[]{:S(2)}, u32[]{:S(2)}) async-start(bf16[64,2,16,128]{3,2,1,0:T(8,128)(2,1)} %sums.1.after_ref), calls=%async_computation.1 | async-start | bytes 1048576 | tf_op jit(solution)/shard_map/all_to_all | solution.py:212

commit v3 on v2

v3 whole, which is shorter than its diff:
```python
import functools
import math

import jax
import jax.numpy as jnp
from jax import lax
from jax.experimental import pallas as pl
from jax.experimental.pallas import tpu as pltpu
from jax.sharding import PartitionSpec as P

HEAD = 128
BLOCK = 512
TILE = 256
F32, BF16 = jnp.float32, jnp.bfloat16
MIB = 1024 * 1024
IN_VMEM = pl.BlockSpec(memory_space=pltpu.VMEM)
ANYWHERE = pl.BlockSpec(memory_space=pl.ANY)


def near(*arrays):
    return [pltpu.with_memory_space_constraint(a, pltpu.VMEM) for a in arrays]


def far(*arrays):
    return [pltpu.with_memory_space_constraint(a, pltpu.HBM) for a in arrays]


def dot(a, b, contract):
    return lax.dot_general(a, b, (((contract[0],), (contract[1],)), ((), ())), preferred_element_type=F32)


def columns(j, size):
    return pl.ds(pl.multiple_of(j * size, size), size)


def spans(length):
    return [pl.ds(i * TILE, TILE) for i in range(length // TILE)]


def put_states(left, right, write):
    for h in range(0, left.shape[1] // HEAD, 2):
        both = slice(h * HEAD, (h + 2) * HEAD)
        product = dot(left[:, both], right[:, both], (0, 0)).astype(BF16)
        write(h, product[:HEAD, :HEAD])
        write(h + 1, product[HEAD:, HEAD:])


def first_kernel(mine_ref, grad_hbm, weight_hbm, key_hbm, value_hbm, query_hbm, part_ref, state_ref, there_ref, query_ref,
                 grad_ref, here_ref, key_ref, value_ref, tile_sem, rest_sem):
    length, width = part_ref.shape
    rows = state_ref.shape[1]
    each = HEAD // rows
    tiles = spans(length)
    mine = mine_ref[0]
    grads, weights, keys, values = [
        [pltpu.make_async_copy(source.at[t, cols], target.at[t, :], tile_sem.at[n, i]) for i, t in enumerate(tiles)]
        for n, (source, target, cols) in enumerate(
            (
                (grad_hbm, grad_ref, slice(None)),
                (weight_hbm, here_ref, columns(mine, width)),
                (key_hbm, key_ref, slice(None)),
                (value_hbm, value_ref, slice(None)),
            )
        )
    ]
    rest = [
        pltpu.make_async_copy(weight_hbm.at[:, columns(1 - mine, width)], there_ref, rest_sem.at[0]),
        pltpu.make_async_copy(query_hbm, query_ref, rest_sem.at[1]),
    ]
    for copy in [grads[0], *weights, *grads[1:], *keys, *values, *rest]:
        copy.start()
    for copy in weights:
        copy.wait()
    for copy, t in zip(grads, tiles):
        copy.wait()
        part_ref[t, :] = dot(grad_ref[t, :], here_ref[...], (1, 1))
    for copy in [*keys, *values]:
        copy.wait()

    def write(h, state):
        state_ref[h * each : (h + 1) * each] = state.reshape(each, rows, HEAD)

    put_states(key_ref, value_ref, write)
    for copy in rest:
        copy.wait()


def second_kernel(grad_ref, weight_ref, part_ref, query_ref, state_ref, head_hbm, sent_ref, head_ref, sem):
    rows = state_ref.shape[1]
    each = HEAD // rows
    copies = []
    for i, t in enumerate(spans(part_ref.shape[0])):
        head_ref[t, :] = (part_ref[t, :] + dot(grad_ref[t, :], weight_ref[...], (1, 1))).astype(BF16)
        copies.append(pltpu.make_async_copy(head_ref.at[t, :], head_hbm.at[t, :], sem.at[i]))
        copies[-1].start()
    sent_ref[:, 0] = state_ref[...]

    def write(h, state):
        sent_ref[h * each : (h + 1) * each, 1] = state.reshape(each, rows, HEAD)

    put_states(query_ref, head_ref, write)
    for copy in copies:
        copy.wait()


def inner_kernel(factor, after_ref, query_ref, key_ref, value_ref, head_ref, dq_ref, dk_ref, dv_ref):
    del after_ref
    blocks = query_ref.shape[0] // BLOCK
    later = lax.broadcasted_iota(jnp.int32, (BLOCK, BLOCK), 0)
    earlier = lax.broadcasted_iota(jnp.int32, (BLOCK, BLOCK), 1)
    causal = earlier <= later
    parts = [pl.ds(b * BLOCK, BLOCK) for b in range(blocks)]
    before, after = [None] * blocks, [None] * blocks
    for b in range(1, blocks):
        state = dot(key_ref[parts[b - 1], :], value_ref[parts[b - 1], :], (0, 0))
        before[b] = state if b == 1 else before[b - 1] + state
    for b in reversed(range(blocks - 1)):
        state = dot(query_ref[parts[b + 1], :], head_ref[parts[b + 1], :], (0, 0))
        after[b] = state if b == blocks - 2 else after[b + 1] + state
    for b, at in enumerate(parts):
        q, k, v, g = query_ref[at, :], key_ref[at, :], value_ref[at, :], head_ref[at, :]
        probs = jnp.where(causal, factor * dot(q, k, (1, 1)), 0.0).astype(BF16)
        weight = jnp.where(causal, factor * dot(g, v, (1, 1)), 0.0).astype(BF16)
        dq, dk, dv = dot(weight, k, (1, 0)), dot(weight, q, (0, 0)), dot(probs, g, (0, 0))
        if before[b] is not None:
            dq = dq + dot(g, (factor * before[b]).astype(BF16), (1, 1))
        if after[b] is not None:
            low = (factor * after[b]).astype(BF16)
            dk = dk + dot(v, low, (1, 1))
            dv = dv + dot(k, low, (1, 0))
        for ref, value in ((dq_ref, dq), (dk_ref, dk), (dv_ref, dv)):
            out = slice(None) if ref.shape[1] == HEAD else columns(pl.program_id(0), HEAD)
            ref[at, out] = value.astype(BF16)


def middle_kernel(factor, given_ref, after_ref, carried_ref):
    del after_ref
    count, _, rows, width = given_ref.shape
    total = jnp.zeros((rows, width), F32)
    for i in range(count):
        carried_ref[i, 0] = (factor * total).astype(BF16)
        total = total + given_ref[i, 0].astype(F32)
    total = jnp.zeros((rows, width), F32)
    for i in reversed(range(count)):
        carried_ref[i, 1] = (factor * total).astype(BF16)
        total = total + given_ref[i, 1].astype(F32)


def two_heads(carried_ref, h, which):
    each = HEAD // carried_ref.shape[2]
    one = carried_ref[h * each : (h + 1) * each, which].reshape(HEAD, HEAD)
    two = carried_ref[(h + 1) * each : (h + 2) * each, which].reshape(HEAD, HEAD)
    none = jnp.zeros_like(one)
    return jnp.concatenate([jnp.concatenate([one, none], 1), jnp.concatenate([none, two], 1)], 0)


def last_kernel(carried_ref, key_ref, value_ref, head_ref, *refs):
    (dq_a, dk_a, dv_a, dq_b, dk_b, dv_b), (dq_ref, dk_ref, dv_ref) = refs[:6], refs[6:]
    here = columns(pl.program_id(0), TILE)
    heads = key_ref.shape[1] // HEAD
    for h in range(0, heads, 2):
        col = slice(h * HEAD, (h + 2) * HEAD)
        if h < heads // 2:
            dq_in, dk_in, dv_in = dq_a[:, col], dk_a[:, col], dv_a[:, col]
        else:
            low = slice((h - heads // 2) * HEAD, (h + 2 - heads // 2) * HEAD)
            dq_in, dk_in, dv_in = dq_b[here, low], dk_b[here, low], dv_b[:, low]
        before, after = two_heads(carried_ref, h, 0), two_heads(carried_ref, h, 1)
        dq_ref[:, col] = (dq_in + dot(head_ref[:, col], before, (1, 1))).astype(BF16)
        dk_ref[:, col] = (dk_in + dot(value_ref[:, col], after, (1, 1))).astype(BF16)
        dv_ref[:, col] = (dv_in + dot(key_ref[:, col], after, (1, 0))).astype(BF16)


def per_device(query_rows, key_rows, value_rows, out_grad, out_weight):
    length, width = query_rows.shape
    count = lax.axis_size("ctx")
    heads = width // HEAD
    factor = 1.0 / math.sqrt(HEAD * length * count)
    rows = width // count
    params = pltpu.CompilerParams(vmem_limit_bytes=16 * MIB)
    product = 2 * length * width * width
    area = length * width

    def cost(flops, bytes_accessed):
        return pl.CostEstimate(flops=int(flops), bytes_accessed=int(bytes_accessed), transcendentals=0)

    other_grad = lax.ppermute(out_grad, "head", [(0, 1), (1, 0)])
    mine = lax.axis_index("head").astype(jnp.int32).reshape(1)

    semaphores = pltpu.SemaphoreType.DMA
    tiles = length // TILE
    part, key_state, there, query_near = pl.pallas_call(
        first_kernel,
        in_specs=[pl.BlockSpec(memory_space=pltpu.SMEM)] + [ANYWHERE] * 5,
        out_specs=[IN_VMEM] * 4,
        out_shape=[
            pltpu.VMEM((length, width), F32),
            jax.ShapeDtypeStruct((count, rows, HEAD), BF16),
            pltpu.VMEM((width, width), BF16),
            pltpu.VMEM((length, width), BF16),
        ],
        scratch_shapes=[pltpu.VMEM((length, width), BF16)] * 4 + [semaphores((4, tiles)), semaphores((2,))],
        compiler_params=params,
        cost_estimate=cost(2 * product, 12 * area),
        name="own_part",
    )(mine, *far(out_grad, out_weight, key_rows, value_rows, query_rows))

    head_grad, sent = pl.pallas_call(
        second_kernel,
        in_specs=[IN_VMEM] * 5,
        out_specs=[ANYWHERE, IN_VMEM],
        out_shape=[pltpu.HBM((length, width), BF16), pltpu.VMEM((count, 2, rows, HEAD), BF16)],
        scratch_shapes=[pltpu.VMEM((length, width), BF16), semaphores((tiles,))],
        compiler_params=params,
        cost_estimate=cost(2 * product, 8 * area),
        name="other_part",
    )(*near(other_grad, there, part, query_near, key_state))

    given = lax.all_to_all(sent, "ctx", 0, 0)

    def inner(base, number, after, places):
        return pl.pallas_call(
            functools.partial(inner_kernel, factor),
            grid=(number,),
            in_specs=[ANYWHERE] + [pl.BlockSpec((length, HEAD), lambda h: (0, h + base))] * 4,
            out_specs=[IN_VMEM if p is pltpu.VMEM else pl.BlockSpec((length, HEAD), lambda h: (0, h)) for p in places],
            out_shape=[p((length, number * HEAD), BF16) for p in places],
            compiler_params=params,
            cost_estimate=cost(6 * product * number / heads, 10 * area),
            name=f"inner_{base}",
        )(after, *far(query_rows, key_rows, value_rows, head_grad))

    half = heads // 2
    local_a = inner(0, half, key_state, [pltpu.HBM] * 3)
    carried = pl.pallas_call(
        functools.partial(middle_kernel, factor),
        in_specs=[IN_VMEM, ANYWHERE],
        out_specs=IN_VMEM,
        out_shape=pltpu.VMEM(given.shape, BF16),
        compiler_params=pltpu.CompilerParams(vmem_limit_bytes=4 * MIB),
        name="sums",
    )(*near(given), *far(local_a[0]))
    local_b = inner(half, heads - half, carried, [pltpu.VMEM, pltpu.VMEM, pltpu.HBM])
    carried = lax.all_to_all(carried, "ctx", 0, 0)

    tile = pl.BlockSpec((TILE, width), lambda i: (i, 0))
    half_tile = pl.BlockSpec((TILE, width // 2), lambda i: (i, 0))
    return pl.pallas_call(
        last_kernel,
        grid=(length // TILE,),
        in_specs=[IN_VMEM] + [tile] * 3 + [half_tile] * 3 + [IN_VMEM, IN_VMEM, half_tile],
        out_specs=[tile] * 3,
        out_shape=[jax.ShapeDtypeStruct((length, width), BF16)] * 3,
        compiler_params=params,
        cost_estimate=cost(product, 18 * area),
        name="carried_part",
    )(*near(carried), *far(key_rows, value_rows, head_grad, *local_a), *near(*local_b[:2]), *far(local_b[2]))


def solution(mesh):
    rows = P("ctx", "head")
    return jax.shard_map(
        per_device,
        mesh=mesh,
        in_specs=(rows, rows, rows, rows, P("head", None)),
        out_specs=(rows, rows, rows),
        check_vma=False,
    )
```

time: 68.3 us -> 63.8 us (0.934)
  Pallas kernels: 41.2 us -> 36.6 us
    pallas_call x2, Pallas kernels: 13.4 us -> 9.67 us  [the longest x1 5.57 us: per_device(): pl.pallas_call(first_kernel, in_specs=[pl.BlockSpec(memory_space=pltpu.SM...]
where the time goes in v3:
time: 63.8 us; the launch traced here: 62.7 us
  Pallas kernels  36.6 us (57%)
  starting transfers between devices  19.2 us (30%)
  waiting for transfers between devices  6.17 us (10%)
  between operations  0.67 us (1%)
    pallas_call x2, Pallas kernels, inner(): pl.pallas_call(functools.partial(inner_kernel, factor), grid=(number,), i...  18.5 us
    all_to_all x1, starting transfers between devices, per_device(): given = lax.all_to_all(sent, 'ctx', 0, 0)  11.2 us
    pallas_call x1, Pallas kernels, per_device(): pl.pallas_call(last_kernel, grid=(length // TILE,), in_specs=[IN_VMEM] +...  7.56 us
    all_to_all x1, starting transfers between devices, per_device(): carried = lax.all_to_all(carried, 'ctx', 0, 0)  6.49 us
    pallas_call x1, Pallas kernels, per_device(): pl.pallas_call(first_kernel, in_specs=[pl.BlockSpec(memory_space=pltpu.SM...  5.57 us
    pallas_call x1, Pallas kernels, per_device(): pl.pallas_call(second_kernel, in_specs=[IN_VMEM] * 5, out_specs=[ANYWHERE...  4.09 us
    all_to_all x1, waiting for transfers between devices, per_device(): given = lax.all_to_all(sent, 'ctx', 0, 0)  3.3 us
    all_to_all x1, waiting for transfers between devices, per_device(): carried = lax.all_to_all(carried, 'ctx', 0, 0)  2.87 us
  transfers between devices with their start and end apart: 3, of which 2 were waited for; matrix products, arithmetic and copies ran while one was open for 0% of the time, Pallas kernels for 38%

profile of v3, /device:TPU:1, one launch (start us, length us, event | category | flops | bytes accessed | tf_op | source)
XLA Modules:
  0.0 62.7 jit_solution(3021849476748557321)
XLA Ops:
  0.6 1.5 %collective-permute-start = (bf16[1024,1024]{1,0:T(8,128)(2,1)}, bf16[1024,1024]{1,0:T(8,128)(2,1)S(1)}, u32[]{:S(2)}, u32[]{:S(2)}) collective-permute-start(bf16[1024,1024]{1,0:T(8,128)(2,1)} %grad_hbm.1), channel_id=1, source_target_pairs={{0,1},{1,0},{2,3},{3,2},{4,5},{5,4},{6,7},{7,6},{8,9},{9,8},{10,11... | collective-permute-start | bytes 6291464 | tf_op jit(solution)/shard_map/ppermute | solution.py:187
  2.1 5.6 %own_part.1 = (f32[1024,1024]{1,0:T(8,128)S(1)}, bf16[64,16,128]{2,1,0:T(8,128)(2,1)S(1)}, bf16[1024,1024]{1,0:T(8,128)(2,1)S(1)}, bf16[1024,1024]{1,0:T(8,128)(2,1)S(1)}) custom-call(s32[1]{0:T(128)} %bitcast.mine_ref, bf16[1024,1024]{1,0:T(8,128)(2,1)} %grad_hbm.1, bf16[1024,2048]{1,0:T(8,128)(2,1)} %weight_hbm.1, bf16[1024,1024]{1,0:T(8,128)(2,1)} %key_ref.5, ...), custom_call_target="tpu_custom_call" | custom-call | flops 4294967296 | bytes 12582912 | tf_op jit(solution)/shard_map/own_part/pallas_call | solution.py:192
  7.7 0.0 collective-permute-done.grad_ref
  7.7 4.1 %other_part.1 = (bf16[1024,1024]{1,0:T(8,128)(2,1)}, bf16[64,2,16,128]{3,2,1,0:T(8,128)(2,1)}) custom-call(bf16[1024,1024]{1,0:T(8,128)(2,1)S(1)} %collective-permute-done.grad_ref, bf16[1024,1024]{1,0:T(8,128)(2,1)S(1)} %get-tuple-element.15.weight_ref, f32[1024,1024]{1,0:T(8,128)S(1)} %get-tuple-element.16.part_ref, ...), custom_call_target="tpu_custom_call" | custom-call | flops 4294967296 | bytes 8388608 | tf_op jit(solution)/shard_map/other_part/pallas_call | solution.py:208
  11.8 11.2 %all-to-all-start = ((bf16[64,2,16,128]{3,2,1,0:T(8,128)(2,1)}), bf16[64,2,16,128]{3,2,1,0:T(8,128)(2,1)S(1)}, u32[]{:S(2)}, u32[]{:S(2)}) async-start(bf16[64,2,16,128]{3,2,1,0:T(8,128)(2,1)} %get-tuple-element.19), calls=%async_computation | async-start | bytes 1048576 | tf_op jit(solution)/shard_map/all_to_all | solution.py:219
  23.1 9.3 %inner_0.1 = (bf16[1024,512]{1,0:T(8,128)(2,1)}, bf16[1024,512]{1,0:T(8,128)(2,1)}, bf16[1024,512]{1,0:T(8,128)(2,1)}) custom-call(bf16[64,16,128]{2,1,0:T(8,128)(2,1)S(1)} %get-tuple-element.18.state_ref.after_ref, bf16[1024,1024]{1,0:T(8,128)(2,1)} %query_ref.3, bf16[1024,1024]{1,0:T(8,128)(2,1)} %key_ref.5, bf16[1024,1024]{1,0:T(8,128)(2,1)} %value_ref.5, ...), custom_call_target="tpu_custom_call" | custom-call | flops 6442450944 | bytes 10485760 | tf_op jit(solution)/shard_map/inner_0/pallas_call | solution.py:222
  32.4 3.3 %all-to-all-done.given_ref = bf16[64,2,16,128]{3,2,1,0:T(8,128)(2,1)S(1)} async-done(((bf16[64,2,16,128]{3,2,1,0:T(8,128)(2,1)}), bf16[64,2,16,128]{3,2,1,0:T(8,128)(2,1)S(1)}, u32[]{:S(2)}, u32[]{:S(2)}) %all-to-all-start) | async-done | bytes 524320 | tf_op jit(solution)/shard_map/all_to_all | solution.py:219
  35.7 0.9 %sums.1.after_ref = bf16[64,2,16,128]{3,2,1,0:T(8,128)(2,1)} custom-call(bf16[64,2,16,128]{3,2,1,0:T(8,128)(2,1)S(1)} %all-to-all-done.given_ref, bf16[1024,512]{1,0:T(8,128)(2,1)} %get-tuple-element.21.after_ref.refs_0_), custom_call_target="tpu_custom_call" | custom-call | tf_op jit(solution)/shard_map/sums/pallas_call | solution.py:235
  36.6 6.5 %all-to-all-start.1 = ((bf16[64,2,16,128]{3,2,1,0:T(8,128)(2,1)}), bf16[64,2,16,128]{3,2,1,0:T(8,128)(2,1)S(1)}, u32[]{:S(2)}, u32[]{:S(2)}) async-start(bf16[64,2,16,128]{3,2,1,0:T(8,128)(2,1)} %sums.1.after_ref), calls=%async_computation.1 | async-start | bytes 1048576 | tf_op jit(solution)/shard_map/all_to_all | solution.py:244
  43.1 9.1 %inner_4.1 = (bf16[1024,512]{1,0:T(8,128)(2,1)S(1)}, bf16[1024,512]{1,0:T(8,128)(2,1)S(1)}, bf16[1024,512]{1,0:T(8,128)(2,1)}) custom-call(bf16[64,2,16,128]{3,2,1,0:T(8,128)(2,1)} %sums.1.after_ref, bf16[1024,1024]{1,0:T(8,128)(2,1)} %query_ref.3, bf16[1024,1024]{1,0:T(8,128)(2,1)} %key_ref.5, bf16[1024,1024]{1,0:T(8,128)(2,1)} %value_ref.5, ...), custom_call_target="tpu_custom_call" | custom-call | flops 6442450944 | bytes 10485760 | tf_op jit(solution)/shard_map/inner_4/pallas_call | solution.py:222
  52.2 2.9 %all-to-all-done.1.carried_ref = bf16[64,2,16,128]{3,2,1,0:T(8,128)(2,1)S(1)} async-done(((bf16[64,2,16,128]{3,2,1,0:T(8,128)(2,1)}), bf16[64,2,16,128]{3,2,1,0:T(8,128)(2,1)S(1)}, u32[]{:S(2)}, u32[]{:S(2)}) %all-to-all-start.1) | async-done | bytes 524320 | tf_op jit(solution)/shard_map/all_to_all | solution.py:244
  55.1 7.6 %carried_part.1 = (bf16[1024,1024]{1,0:T(8,128)(2,1)}, bf16[1024,1024]{1,0:T(8,128)(2,1)}, bf16[1024,1024]{1,0:T(8,128)(2,1)}) custom-call(bf16[64,2,16,128]{3,2,1,0:T(8,128)(2,1)S(1)} %all-to-all-done.1.carried_ref, bf16[1024,1024]{1,0:T(8,128)(2,1)} %key_ref.5, bf16[1024,1024]{1,0:T(8,128)(2,1)} %value_ref.5, ...), custom_call_target="tpu_custom_call" | custom-call | flops 2147483648 | bytes 18874368 | tf_op jit(solution)/shard_map/carried_part/pallas_call | solution.py:248
Async XLA Ops:
  0.6 7.1 %collective-permute-start = (bf16[1024,1024]{1,0:T(8,128)(2,1)}, bf16[1024,1024]{1,0:T(8,128)(2,1)S(1)}, u32[]{:S(2)}, u32[]{:S(2)}) collective-permute-start(bf16[1024,1024]{1,0:T(8,128)(2,1)} %grad_hbm.1), channel_id=1, source_target_pairs={{0,1},{1,0},{2,3},{3,2},{4,5},{5,4},{6,7},{7,6},{8,9},{9,8},{10,11... | collective-permute-start | bytes 6291464 | tf_op jit(solution)/shard_map/ppermute | solution.py:187
  11.8 23.9 %all-to-all-start = ((bf16[64,2,16,128]{3,2,1,0:T(8,128)(2,1)}), bf16[64,2,16,128]{3,2,1,0:T(8,128)(2,1)S(1)}, u32[]{:S(2)}, u32[]{:S(2)}) async-start(bf16[64,2,16,128]{3,2,1,0:T(8,128)(2,1)} %get-tuple-element.19), calls=%async_computation | async-start | bytes 1048576 | tf_op jit(solution)/shard_map/all_to_all | solution.py:219
  36.6 18.5 %all-to-all-start.1 = ((bf16[64,2,16,128]{3,2,1,0:T(8,128)(2,1)}), bf16[64,2,16,128]{3,2,1,0:T(8,128)(2,1)S(1)}, u32[]{:S(2)}, u32[]{:S(2)}) async-start(bf16[64,2,16,128]{3,2,1,0:T(8,128)(2,1)} %sums.1.after_ref), calls=%async_computation.1 | async-start | bytes 1048576 | tf_op jit(solution)/shard_map/all_to_all | solution.py:244

commit v4 on v3

--- a/solution.py
+++ b/solution.py
@@ -9,7 +9,8 @@
 from jax.sharding import PartitionSpec as P
 
 HEAD = 128
-BLOCK = 512
+BLOCK = 256
+PAIR = 2 * HEAD
 TILE = 256
 F32, BF16 = jnp.float32, jnp.bfloat16
 MIB = 1024 * 1024
@@ -45,7 +46,7 @@
         write(h + 1, product[HEAD:, HEAD:])
 
 
-def first_kernel(mine_ref, grad_hbm, weight_hbm, key_hbm, value_hbm, query_hbm, part_ref, state_ref, there_ref, query_ref,
+def first_kernel(mine_ref, grad_hbm, weight_hbm, key_hbm, value_hbm, part_ref, state_ref, there_ref,
                  grad_ref, here_ref, key_ref, value_ref, tile_sem, rest_sem):
     length, width = part_ref.shape
     rows = state_ref.shape[1]
@@ -63,11 +64,8 @@
             )
         )
     ]
-    rest = [
-        pltpu.make_async_copy(weight_hbm.at[:, columns(1 - mine, width)], there_ref, rest_sem.at[0]),
-        pltpu.make_async_copy(query_hbm, query_ref, rest_sem.at[1]),
-    ]
-    for copy in [grads[0], *weights, *grads[1:], *keys, *values, *rest]:
+    rest = pltpu.make_async_copy(weight_hbm.at[:, columns(1 - mine, width)], there_ref, rest_sem)
+    for copy in [grads[0], *weights, *grads[1:], *keys, *values, rest]:
         copy.start()
     for copy in weights:
         copy.wait()
@@ -81,13 +79,14 @@
         state_ref[h * each : (h + 1) * each] = state.reshape(each, rows, HEAD)
 
     put_states(key_ref, value_ref, write)
-    for copy in rest:
-        copy.wait()
-
-
-def second_kernel(grad_ref, weight_ref, part_ref, query_ref, state_ref, head_hbm, sent_ref, head_ref, sem):
+    rest.wait()
+
+
+def second_kernel(grad_ref, weight_ref, part_ref, query_hbm, state_ref, head_hbm, sent_ref, query_ref, head_ref, sem, query_sem):
     rows = state_ref.shape[1]
     each = HEAD // rows
+    fetch = pltpu.make_async_copy(query_hbm, query_ref, query_sem)
+    fetch.start()
     copies = []
     for i, t in enumerate(spans(part_ref.shape[0])):
         head_ref[t, :] = (part_ref[t, :] + dot(grad_ref[t, :], weight_ref[...], (1, 1))).astype(BF16)
@@ -98,6 +97,7 @@
     def write(h, state):
         sent_ref[h * each : (h + 1) * each, 1] = state.reshape(each, rows, HEAD)
 
+    fetch.wait()
     put_states(query_ref, head_ref, write)
     for copy in copies:
         copy.wait()
@@ -106,10 +106,18 @@
 def inner_kernel(factor, after_ref, query_ref, key_ref, value_ref, head_ref, dq_ref, dk_ref, dv_ref):
     del after_ref
     blocks = query_ref.shape[0] // BLOCK
-    later = lax.broadcasted_iota(jnp.int32, (BLOCK, BLOCK), 0)
-    earlier = lax.broadcasted_iota(jnp.int32, (BLOCK, BLOCK), 1)
-    causal = earlier <= later
+    down = lax.broadcasted_iota(jnp.int32, (BLOCK, BLOCK), 0)
+    across = lax.broadcasted_iota(jnp.int32, (BLOCK, BLOCK), 1)
+    left_head = lax.broadcasted_iota(jnp.int32, (PAIR, PAIR), 0) < HEAD
+    same_head = left_head == (lax.broadcasted_iota(jnp.int32, (PAIR, PAIR), 1) < HEAD)
     parts = [pl.ds(b * BLOCK, BLOCK) for b in range(blocks)]
+
+    def lowered(state):
+        return jnp.where(same_head, factor * state, 0.0).astype(BF16)
+
+    def scores(keep, left, right):
+        return jnp.where(keep, factor * dot(left, right, (1, 1)), 0.0).astype(BF16)
+
     before, after = [None] * blocks, [None] * blocks
     for b in range(1, blocks):
         state = dot(key_ref[parts[b - 1], :], value_ref[parts[b - 1], :], (0, 0))
@@ -118,19 +126,25 @@
         state = dot(query_ref[parts[b + 1], :], head_ref[parts[b + 1], :], (0, 0))
         after[b] = state if b == blocks - 2 else after[b + 1] + state
     for b, at in enumerate(parts):
-        q, k, v, g = query_ref[at, :], key_ref[at, :], value_ref[at, :], head_ref[at, :]
-        probs = jnp.where(causal, factor * dot(q, k, (1, 1)), 0.0).astype(BF16)
-        weight = jnp.where(causal, factor * dot(g, v, (1, 1)), 0.0).astype(BF16)
-        dq, dk, dv = dot(weight, k, (1, 0)), dot(weight, q, (0, 0)), dot(probs, g, (0, 0))
+        sums = [None] * 3
         if before[b] is not None:
-            dq = dq + dot(g, (factor * before[b]).astype(BF16), (1, 1))
+            sums[0] = dot(head_ref[at, :], lowered(before[b]), (1, 1))
         if after[b] is not None:
-            low = (factor * after[b]).astype(BF16)
-            dk = dk + dot(v, low, (1, 1))
-            dv = dv + dot(k, low, (1, 0))
-        for ref, value in ((dq_ref, dq), (dk_ref, dk), (dv_ref, dv)):
-            out = slice(None) if ref.shape[1] == HEAD else columns(pl.program_id(0), HEAD)
-            ref[at, out] = value.astype(BF16)
+            low = lowered(after[b])
+            sums[1:] = dot(value_ref[at, :], low, (1, 1)), dot(key_ref[at, :], low, (1, 0))
+        for h in range(2):
+            col = slice(h * HEAD, (h + 1) * HEAD)
+            q, k, v, g = query_ref[at, col], key_ref[at, col], value_ref[at, col], head_ref[at, col]
+            values = [
+                dot(scores(across <= down, g, v), k, (1, 0)),
+                dot(scores(down <= across, v, g), q, (1, 0)),
+                dot(scores(down <= across, k, q), g, (1, 0)),
+            ]
+            for ref, value, extra in zip((dq_ref, dk_ref, dv_ref), values, sums):
+                if extra is not None:
+                    value = value + extra[:, col]
+                out = col if ref.shape[1] == PAIR else columns(2 * pl.program_id(0) + h, HEAD)
+                ref[at, out] = value.astype(BF16)
 
 
 def middle_kernel(factor, given_ref, after_ref, carried_ref):
@@ -154,21 +168,42 @@
     return jnp.concatenate([jnp.concatenate([one, none], 1), jnp.concatenate([none, two], 1)], 0)
 
 
-def last_kernel(carried_ref, key_ref, value_ref, head_ref, *refs):
-    (dq_a, dk_a, dv_a, dq_b, dk_b, dv_b), (dq_ref, dk_ref, dv_ref) = refs[:6], refs[6:]
-    here = columns(pl.program_id(0), TILE)
-    heads = key_ref.shape[1] // HEAD
-    for h in range(0, heads, 2):
-        col = slice(h * HEAD, (h + 2) * HEAD)
-        if h < heads // 2:
-            dq_in, dk_in, dv_in = dq_a[:, col], dk_a[:, col], dv_a[:, col]
-        else:
-            low = slice((h - heads // 2) * HEAD, (h + 2 - heads // 2) * HEAD)
-            dq_in, dk_in, dv_in = dq_b[here, low], dk_b[here, low], dv_b[:, low]
-        before, after = two_heads(carried_ref, h, 0), two_heads(carried_ref, h, 1)
-        dq_ref[:, col] = (dq_in + dot(head_ref[:, col], before, (1, 1))).astype(BF16)
-        dk_ref[:, col] = (dk_in + dot(value_ref[:, col], after, (1, 1))).astype(BF16)
-        dv_ref[:, col] = (dv_in + dot(key_ref[:, col], after, (1, 0))).astype(BF16)
+def last_kernel(carried_ref, key_hbm, value_hbm, head_hbm, dq_a, dk_a, dv_a, dq_b, dk_b, dv_b, dq_hbm, dk_hbm, dv_hbm, *refs):
+    inputs, outputs, (sem, out_sem) = refs[:7], refs[7:10], refs[10:]
+    sources, targets = (head_hbm, dq_a, value_hbm, dk_a, key_hbm, dv_a, dv_b), (dq_hbm, dk_hbm, dv_hbm)
+    length, width = outputs[0].shape
+    edges = [0, TILE // 2, *range(TILE // 2 + TILE, length, TILE), length]
+    tiles = [pl.ds(a, b - a) for a, b in zip(edges, edges[1:])]
+    loads = [
+        [pltpu.make_async_copy(a.at[t, :], b.at[t, :], sem.at[n, i]) for n, (a, b) in enumerate(zip(sources, inputs))]
+        for i, t in enumerate(tiles)
+    ]
+    stores = [
+        [pltpu.make_async_copy(a.at[t, :], b.at[t, :], out_sem.at[n, i]) for n, (a, b) in enumerate(zip(outputs, targets))]
+        for i, t in enumerate(tiles)
+    ]
+    for copy in sum(loads, []):
+        copy.start()
+    states = [(two_heads(carried_ref, h, 0), two_heads(carried_ref, h, 1)) for h in range(0, width // HEAD, 2)]
+    half = width // 2
+    grads, dq_in, values, dk_in, keys, dv_in, dv_rest = inputs
+    for i, t in enumerate(tiles):
+        for copy in loads[i]:
+            copy.wait()
+        for j, (before, after) in enumerate(states):
+            col = slice(j * PAIR, (j + 1) * PAIR)
+            if j * PAIR < half:
+                locals_ = dq_in[t, col], dk_in[t, col], dv_in[t, col]
+            else:
+                low = slice(j * PAIR - half, (j + 1) * PAIR - half)
+                locals_ = dq_b[t, low], dk_b[t, low], dv_rest[t, low]
+            sums = dot(grads[t, col], before, (1, 1)), dot(values[t, col], after, (1, 1)), dot(keys[t, col], after, (1, 0))
+            for ref, own, carried in zip(outputs, locals_, sums):
+                ref[t, col] = (own + carried).astype(BF16)
+        for copy in stores[i]:
+            copy.start()
+    for copy in sum(stores, []):
+        copy.wait()
 
 
 def per_device(query_rows, key_rows, value_rows, out_grad, out_weight):
@@ -189,41 +224,40 @@
 
     semaphores = pltpu.SemaphoreType.DMA
     tiles = length // TILE
-    part, key_state, there, query_near = pl.pallas_call(
+    part, key_state, there = pl.pallas_call(
         first_kernel,
-        in_specs=[pl.BlockSpec(memory_space=pltpu.SMEM)] + [ANYWHERE] * 5,
-        out_specs=[IN_VMEM] * 4,
+        in_specs=[pl.BlockSpec(memory_space=pltpu.SMEM)] + [ANYWHERE] * 4,
+        out_specs=[IN_VMEM] * 3,
         out_shape=[
             pltpu.VMEM((length, width), F32),
             jax.ShapeDtypeStruct((count, rows, HEAD), BF16),
             pltpu.VMEM((width, width), BF16),
-            pltpu.VMEM((length, width), BF16),
         ],
-        scratch_shapes=[pltpu.VMEM((length, width), BF16)] * 4 + [semaphores((4, tiles)), semaphores((2,))],
+        scratch_shapes=[pltpu.VMEM((length, width), BF16)] * 4 + [semaphores((4, tiles)), semaphores],
         compiler_params=params,
         cost_estimate=cost(2 * product, 12 * area),
         name="own_part",
-    )(mine, *far(out_grad, out_weight, key_rows, value_rows, query_rows))
+    )(mine, *far(out_grad, out_weight, key_rows, value_rows))
 
     head_grad, sent = pl.pallas_call(
         second_kernel,
-        in_specs=[IN_VMEM] * 5,
+        in_specs=[IN_VMEM] * 3 + [ANYWHERE, IN_VMEM],
         out_specs=[ANYWHERE, IN_VMEM],
         out_shape=[pltpu.HBM((length, width), BF16), pltpu.VMEM((count, 2, rows, HEAD), BF16)],
-        scratch_shapes=[pltpu.VMEM((length, width), BF16), semaphores((tiles,))],
+        scratch_shapes=[pltpu.VMEM((length, width), BF16)] * 2 + [semaphores((tiles,)), semaphores],
         compiler_params=params,
         cost_estimate=cost(2 * product, 8 * area),
         name="other_part",
-    )(*near(other_grad, there, part, query_near, key_state))
+    )(*near(other_grad, there, part), *far(query_rows), *near(key_state))
 
     given = lax.all_to_all(sent, "ctx", 0, 0)
 
     def inner(base, number, after, places):
         return pl.pallas_call(
             functools.partial(inner_kernel, factor),
-            grid=(number,),
-            in_specs=[ANYWHERE] + [pl.BlockSpec((length, HEAD), lambda h: (0, h + base))] * 4,
-            out_specs=[IN_VMEM if p is pltpu.VMEM else pl.BlockSpec((length, HEAD), lambda h: (0, h)) for p in places],
+            grid=(number // 2,),
+            in_specs=[ANYWHERE] + [pl.BlockSpec((length, PAIR), lambda h: (0, h + base // 2))] * 4,
+            out_specs=[IN_VMEM if p is pltpu.VMEM else pl.BlockSpec((length, PAIR), lambda h: (0, h)) for p in places],
             out_shape=[p((length, number * HEAD), BF16) for p in places],
             compiler_params=params,
             cost_estimate=cost(6 * product * number / heads, 10 * area),
@@ -243,15 +277,16 @@
     local_b = inner(half, heads - half, carried, [pltpu.VMEM, pltpu.VMEM, pltpu.HBM])
     carried = lax.all_to_all(carried, "ctx", 0, 0)
 
-    tile = pl.BlockSpec((TILE, width), lambda i: (i, 0))
-    half_tile = pl.BlockSpec((TILE, width // 2), lambda i: (i, 0))
+    full, part_width = pltpu.VMEM((length, width), BF16), pltpu.VMEM((length, width // 2), BF16)
+    steps = tiles + 1
     return pl.pallas_call(
         last_kernel,
-        grid=(length // TILE,),
-        in_specs=[IN_VMEM] + [tile] * 3 + [half_tile] * 3 + [IN_VMEM, IN_VMEM, half_tile],
-        out_specs=[tile] * 3,
+        in_specs=[IN_VMEM] + [ANYWHERE] * 6 + [IN_VMEM] * 2 + [ANYWHERE],
+        out_specs=[ANYWHERE] * 3,
         out_shape=[jax.ShapeDtypeStruct((length, width), BF16)] * 3,
-        compiler_params=params,
+        scratch_shapes=[full, part_width, full, part_width, full, part_width, part_width, full, full, full]
+        + [semaphores((7, steps)), semaphores((3, steps))],
+        compiler_params=pltpu.CompilerParams(vmem_limit_bytes=24 * MIB),
         cost_estimate=cost(product, 18 * area),
         name="carried_part",
     )(*near(carried), *far(key_rows, value_rows, head_grad, *local_a), *near(*local_b[:2]), *far(local_b[2]))

time: 63.8 us -> 62.6 us (0.981)
  Pallas kernels: 36.6 us -> 34.4 us
  waiting for transfers between devices: 6.17 us -> 7.83 us
  starting transfers between devices: 19.2 us -> 18.5 us
    pallas_call x4, Pallas kernels: 30.1 us -> 27.9 us  [the longest x2 16.6 us: inner(): pl.pallas_call(functools.partial(inner_kernel, factor), grid=(number // 2...]
    all_to_all x1, waiting for transfers between devices: 3.3 us -> 4.19 us  [per_device(): given = lax.all_to_all(sent, 'ctx', 0, 0)]
    all_to_all x1, waiting for transfers between devices: 2.87 us -> 3.64 us  [per_device(): carried = lax.all_to_all(carried, 'ctx', 0, 0)]
    all_to_all x1, starting transfers between devices: 6.49 us -> 5.77 us  [per_device(): carried = lax.all_to_all(carried, 'ctx', 0, 0)]
  transfers between devices with their start and end apart: 3 -> 3, of which waited for: 2 -> 2; matrix products, arithmetic and copies ran while one was open for 0% -> 0% of each run, Pallas kernels for 38% -> 36%
where the time goes in v4:
time: 62.6 us; the launch traced here: 61.5 us
  Pallas kernels  34.4 us (55%)
  starting transfers between devices  18.5 us (30%)
  waiting for transfers between devices  7.83 us (13%)
  between operations  0.83 us (1%)
    pallas_call x2, Pallas kernels, inner(): pl.pallas_call(functools.partial(inner_kernel, factor), grid=(number // 2...  16.6 us
    all_to_all x1, starting transfers between devices, per_device(): given = lax.all_to_all(sent, 'ctx', 0, 0)  11.2 us
    pallas_call x1, Pallas kernels, per_device(): pl.pallas_call(last_kernel, in_specs=[IN_VMEM] + [ANYWHERE] * 6 + [IN_VME...  7.19 us
    all_to_all x1, starting transfers between devices, per_device(): carried = lax.all_to_all(carried, 'ctx', 0, 0)  5.77 us
    pallas_call x1, Pallas kernels, per_device(): pl.pallas_call(first_kernel, in_specs=[pl.BlockSpec(memory_space=pltpu.SM...  5.56 us
    all_to_all x1, waiting for transfers between devices, per_device(): given = lax.all_to_all(sent, 'ctx', 0, 0)  4.19 us
    pallas_call x1, Pallas kernels, per_device(): pl.pallas_call(second_kernel, in_specs=[IN_VMEM] * 3 + [ANYWHERE, IN_VMEM...  4.06 us
    all_to_all x1, waiting for transfers between devices, per_device(): carried = lax.all_to_all(carried, 'ctx', 0, 0)  3.64 us
  transfers between devices with their start and end apart: 3, of which 2 were waited for; matrix products, arithmetic and copies ran while one was open for 0% of the time, Pallas kernels for 36%

profile of v4, /device:TPU:1, one launch (start us, length us, event | category | flops | bytes accessed | tf_op | source)
XLA Modules:
  0.0 61.5 jit_solution(4969030269911859930)
XLA Ops:
  0.6 1.5 %collective-permute-start = (bf16[1024,1024]{1,0:T(8,128)(2,1)}, bf16[1024,1024]{1,0:T(8,128)(2,1)S(1)}, u32[]{:S(2)}, u32[]{:S(2)}) collective-permute-start(bf16[1024,1024]{1,0:T(8,128)(2,1)} %grad_hbm.1), channel_id=1, source_target_pairs={{0,1},{1,0},{2,3},{3,2},{4,5},{5,4},{6,7},{7,6},{8,9},{9,8},{10,11... | collective-permute-start | bytes 6291464 | tf_op jit(solution)/shard_map/ppermute | solution.py:222
  2.1 5.6 %own_part.1 = (f32[1024,1024]{1,0:T(8,128)S(1)}, bf16[64,16,128]{2,1,0:T(8,128)(2,1)S(1)}, bf16[1024,1024]{1,0:T(8,128)(2,1)S(1)}) custom-call(s32[1]{0:T(128)} %bitcast.mine_ref, bf16[1024,1024]{1,0:T(8,128)(2,1)} %grad_hbm.1, bf16[1024,2048]{1,0:T(8,128)(2,1)} %weight_hbm.1, bf16[1024,1024]{1,0:T(8,128)(2,1)} %key_hbm.3, bf16[1024,1024]{1,0:T(8,128)(2,1)} %value_hbm.3), custom_call_target="tpu_custom_call" | custom-call | flops 4294967296 | bytes 12582912 | tf_op jit(solution)/shard_map/own_part/pallas_call | solution.py:227
  7.7 0.0 collective-permute-done.grad_ref
  7.7 4.1 %other_part.1 = (bf16[1024,1024]{1,0:T(8,128)(2,1)}, bf16[64,2,16,128]{3,2,1,0:T(8,128)(2,1)}) custom-call(bf16[1024,1024]{1,0:T(8,128)(2,1)S(1)} %collective-permute-done.grad_ref, bf16[1024,1024]{1,0:T(8,128)(2,1)S(1)} %get-tuple-element.14.weight_ref, f32[1024,1024]{1,0:T(8,128)S(1)} %get-tuple-element.15.part_ref, bf16[1024,1024]{1,0:T(8,128)(2,1)} %query_ref.3, ...), custom_call_target="tpu_custom_call" | custom-call | flops 4294967296 | bytes 8388608 | tf_op jit(solution)/shard_map/other_part/pallas_call | solution.py:242
  11.8 11.2 %all-to-all-start = ((bf16[64,2,16,128]{3,2,1,0:T(8,128)(2,1)}), bf16[64,2,16,128]{3,2,1,0:T(8,128)(2,1)S(1)}, u32[]{:S(2)}, u32[]{:S(2)}) async-start(bf16[64,2,16,128]{3,2,1,0:T(8,128)(2,1)} %get-tuple-element.17), calls=%async_computation | async-start | bytes 1048576 | tf_op jit(solution)/shard_map/all_to_all | solution.py:253
  23.0 8.4 %inner_0.1 = (bf16[1024,512]{1,0:T(8,128)(2,1)}, bf16[1024,512]{1,0:T(8,128)(2,1)}, bf16[1024,512]{1,0:T(8,128)(2,1)}) custom-call(bf16[64,16,128]{2,1,0:T(8,128)(2,1)S(1)} %get-tuple-element.16.state_ref.after_ref, bf16[1024,1024]{1,0:T(8,128)(2,1)} %query_ref.3, bf16[1024,1024]{1,0:T(8,128)(2,1)} %key_hbm.3, bf16[1024,1024]{1,0:T(8,128)(2,1)} %value_hbm.3, ...), custom_call_target="tpu_custom_call" | custom-call | flops 6442450944 | bytes 10485760 | tf_op jit(solution)/shard_map/inner_0/pallas_call | solution.py:256
  31.5 4.2 %all-to-all-done.given_ref = bf16[64,2,16,128]{3,2,1,0:T(8,128)(2,1)S(1)} async-done(((bf16[64,2,16,128]{3,2,1,0:T(8,128)(2,1)}), bf16[64,2,16,128]{3,2,1,0:T(8,128)(2,1)S(1)}, u32[]{:S(2)}, u32[]{:S(2)}) %all-to-all-start) | async-done | bytes 524320 | tf_op jit(solution)/shard_map/all_to_all | solution.py:253
  35.6 0.9 %sums.1.after_ref = bf16[64,2,16,128]{3,2,1,0:T(8,128)(2,1)} custom-call(bf16[64,2,16,128]{3,2,1,0:T(8,128)(2,1)S(1)} %all-to-all-done.given_ref, bf16[1024,512]{1,0:T(8,128)(2,1)} %get-tuple-element.19.after_ref.dq_a), custom_call_target="tpu_custom_call" | custom-call | tf_op jit(solution)/shard_map/sums/pallas_call | solution.py:269
  36.6 5.8 %all-to-all-start.1 = ((bf16[64,2,16,128]{3,2,1,0:T(8,128)(2,1)}), bf16[64,2,16,128]{3,2,1,0:T(8,128)(2,1)S(1)}, u32[]{:S(2)}, u32[]{:S(2)}) async-start(bf16[64,2,16,128]{3,2,1,0:T(8,128)(2,1)} %sums.1.after_ref), calls=%async_computation.1 | async-start | bytes 1048576 | tf_op jit(solution)/shard_map/all_to_all | solution.py:278
  42.3 8.2 %inner_4.1 = (bf16[1024,512]{1,0:T(8,128)(2,1)S(1)}, bf16[1024,512]{1,0:T(8,128)(2,1)S(1)}, bf16[1024,512]{1,0:T(8,128)(2,1)}) custom-call(bf16[64,2,16,128]{3,2,1,0:T(8,128)(2,1)} %sums.1.after_ref, bf16[1024,1024]{1,0:T(8,128)(2,1)} %query_ref.3, bf16[1024,1024]{1,0:T(8,128)(2,1)} %key_hbm.3, bf16[1024,1024]{1,0:T(8,128)(2,1)} %value_hbm.3, ...), custom_call_target="tpu_custom_call" | custom-call | flops 6442450944 | bytes 10485760 | tf_op jit(solution)/shard_map/inner_4/pallas_call | solution.py:256
  50.5 3.6 %all-to-all-done.1.carried_ref = bf16[64,2,16,128]{3,2,1,0:T(8,128)(2,1)S(1)} async-done(((bf16[64,2,16,128]{3,2,1,0:T(8,128)(2,1)}), bf16[64,2,16,128]{3,2,1,0:T(8,128)(2,1)S(1)}, u32[]{:S(2)}, u32[]{:S(2)}) %all-to-all-start.1) | async-done | bytes 524320 | tf_op jit(solution)/shard_map/all_to_all | solution.py:278
  54.2 7.2 %carried_part.1 = (bf16[1024,1024]{1,0:T(8,128)(2,1)}, bf16[1024,1024]{1,0:T(8,128)(2,1)}, bf16[1024,1024]{1,0:T(8,128)(2,1)}) custom-call(bf16[64,2,16,128]{3,2,1,0:T(8,128)(2,1)S(1)} %all-to-all-done.1.carried_ref, bf16[1024,1024]{1,0:T(8,128)(2,1)} %key_hbm.3, bf16[1024,1024]{1,0:T(8,128)(2,1)} %value_hbm.3, ...), custom_call_target="tpu_custom_call" | custom-call | flops 2147483648 | bytes 18874368 | tf_op jit(solution)/shard_map/carried_part/pallas_call | solution.py:282
Async XLA Ops:
  0.6 7.1 %collective-permute-start = (bf16[1024,1024]{1,0:T(8,128)(2,1)}, bf16[1024,1024]{1,0:T(8,128)(2,1)S(1)}, u32[]{:S(2)}, u32[]{:S(2)}) collective-permute-start(bf16[1024,1024]{1,0:T(8,128)(2,1)} %grad_hbm.1), channel_id=1, source_target_pairs={{0,1},{1,0},{2,3},{3,2},{4,5},{5,4},{6,7},{7,6},{8,9},{9,8},{10,11... | collective-permute-start | bytes 6291464 | tf_op jit(solution)/shard_map/ppermute | solution.py:222
  11.8 23.9 %all-to-all-start = ((bf16[64,2,16,128]{3,2,1,0:T(8,128)(2,1)}), bf16[64,2,16,128]{3,2,1,0:T(8,128)(2,1)S(1)}, u32[]{:S(2)}, u32[]{:S(2)}) async-start(bf16[64,2,16,128]{3,2,1,0:T(8,128)(2,1)} %get-tuple-element.17), calls=%async_computation | async-start | bytes 1048576 | tf_op jit(solution)/shard_map/all_to_all | solution.py:253
  36.6 17.6 %all-to-all-start.1 = ((bf16[64,2,16,128]{3,2,1,0:T(8,128)(2,1)}), bf16[64,2,16,128]{3,2,1,0:T(8,128)(2,1)S(1)}, u32[]{:S(2)}, u32[]{:S(2)}) async-start(bf16[64,2,16,128]{3,2,1,0:T(8,128)(2,1)} %sums.1.after_ref), calls=%async_computation.1 | async-start | bytes 1048576 | tf_op jit(solution)/shard_map/all_to_all | solution.py:278

commit v5 on v4

--- a/solution.py
+++ b/solution.py
@@ -103,7 +103,7 @@
         copy.wait()
 
 
-def inner_kernel(factor, after_ref, query_ref, key_ref, value_ref, head_ref, dq_ref, dk_ref, dv_ref):
+def inner_kernel(factor, after_ref, query_ref, key_ref, value_ref, head_ref, dq_ref, dk_ref, dv_ref, before_ref, behind_ref):
     del after_ref
     blocks = query_ref.shape[0] // BLOCK
     down = lax.broadcasted_iota(jnp.int32, (BLOCK, BLOCK), 0)
@@ -118,19 +118,22 @@
     def scores(keep, left, right):
         return jnp.where(keep, factor * dot(left, right, (1, 1)), 0.0).astype(BF16)
 
-    before, after = [None] * blocks, [None] * blocks
+    state = None
     for b in range(1, blocks):
-        state = dot(key_ref[parts[b - 1], :], value_ref[parts[b - 1], :], (0, 0))
-        before[b] = state if b == 1 else before[b - 1] + state
+        step = dot(key_ref[parts[b - 1], :], value_ref[parts[b - 1], :], (0, 0))
+        state = step if state is None else state + step
+        before_ref[b] = lowered(state)
+    state = None
     for b in reversed(range(blocks - 1)):
-        state = dot(query_ref[parts[b + 1], :], head_ref[parts[b + 1], :], (0, 0))
-        after[b] = state if b == blocks - 2 else after[b + 1] + state
+        step = dot(query_ref[parts[b + 1], :], head_ref[parts[b + 1], :], (0, 0))
+        state = step if state is None else state + step
+        behind_ref[b] = lowered(state)
     for b, at in enumerate(parts):
         sums = [None] * 3
-        if before[b] is not None:
-            sums[0] = dot(head_ref[at, :], lowered(before[b]), (1, 1))
-        if after[b] is not None:
-            low = lowered(after[b])
+        if b > 0:
+            sums[0] = dot(head_ref[at, :], before_ref[b], (1, 1))
+        if b < blocks - 1:
+            low = behind_ref[b]
             sums[1:] = dot(value_ref[at, :], low, (1, 1)), dot(key_ref[at, :], low, (1, 0))
         for h in range(2):
             col = slice(h * HEAD, (h + 1) * HEAD)
@@ -151,11 +154,11 @@
     del after_ref
     count, _, rows, width = given_ref.shape
     total = jnp.zeros((rows, width), F32)
-    for i in range(count):
+    for i in reversed(range(count)):
         carried_ref[i, 0] = (factor * total).astype(BF16)
         total = total + given_ref[i, 0].astype(F32)
     total = jnp.zeros((rows, width), F32)
-    for i in reversed(range(count)):
+    for i in range(count):
         carried_ref[i, 1] = (factor * total).astype(BF16)
         total = total + given_ref[i, 1].astype(F32)
 
@@ -209,6 +212,7 @@
 def per_device(query_rows, key_rows, value_rows, out_grad, out_weight):
     length, width = query_rows.shape
     count = lax.axis_size("ctx")
+    order = [list(reversed(range(count)))]
     heads = width // HEAD
     factor = 1.0 / math.sqrt(HEAD * length * count)
     rows = width // count
@@ -250,7 +254,7 @@
         name="other_part",
     )(*near(other_grad, there, part), *far(query_rows), *near(key_state))
 
-    given = lax.all_to_all(sent, "ctx", 0, 0)
+    given = lax.all_to_all(sent, "ctx", 0, 0, axis_index_groups=order)
 
     def inner(base, number, after, places):
         return pl.pallas_call(
@@ -259,6 +263,7 @@
             in_specs=[ANYWHERE] + [pl.BlockSpec((length, PAIR), lambda h: (0, h + base // 2))] * 4,
             out_specs=[IN_VMEM if p is pltpu.VMEM else pl.BlockSpec((length, PAIR), lambda h: (0, h)) for p in places],
             out_shape=[p((length, number * HEAD), BF16) for p in places],
+            scratch_shapes=[pltpu.VMEM((length // BLOCK, PAIR, PAIR), BF16)] * 2,
             compiler_params=params,
             cost_estimate=cost(6 * product * number / heads, 10 * area),
             name=f"inner_{base}",
@@ -275,7 +280,7 @@
         name="sums",
     )(*near(given), *far(local_a[0]))
     local_b = inner(half, heads - half, carried, [pltpu.VMEM, pltpu.VMEM, pltpu.HBM])
-    carried = lax.all_to_all(carried, "ctx", 0, 0)
+    carried = lax.all_to_all(carried, "ctx", 0, 0, axis_index_groups=order)
 
     full, part_width = pltpu.VMEM((length, width), BF16), pltpu.VMEM((length, width // 2), BF16)
     steps = tiles + 1

time: 62.6 us -> 59.7 us (0.954); the launches traced: 61.5 us -> 59.4 us
  waiting for transfers between devices: 7.83 us -> 0.01 us
  starting transfers between devices: 18.5 us -> 24.3 us
    all_to_all x2, waiting for transfers between devices: 7.82 us -> 0.01 us  [the longest x1 0.01 us: per_device(): given = lax.all_to_all(sent, 'ctx', 0, 0, axis_index_groups=order)]
    all_to_all x2, starting transfers between devices: 17 us -> 22.8 us  [the longest x1 13 us: per_device(): given = lax.all_to_all(sent, 'ctx', 0, 0, axis_index_groups=order)]
  transfers between devices with their start and end apart: 3 -> 3, of which waited for: 2 -> 0; matrix products, arithmetic and copies ran while one was open for 0% -> 0% of each run, Pallas kernels for 36% -> 37%
where the time goes in v5:
time: 59.7 us; the launch traced here: 59.4 us
  Pallas kernels  34.3 us (57%)
  starting transfers between devices  24.3 us (41%)
  between operations  0.83 us (1%)
    pallas_call x2, Pallas kernels, inner(): pl.pallas_call(functools.partial(inner_kernel, factor), grid=(number // 2...  16.6 us
    all_to_all x1, starting transfers between devices, per_device(): given = lax.all_to_all(sent, 'ctx', 0, 0, axis_index_groups=order)  13 us
    all_to_all x1, starting transfers between devices, per_device(): carried = lax.all_to_all(carried, 'ctx', 0, 0, axis_index_groups=order)  9.79 us
    pallas_call x1, Pallas kernels, per_device(): pl.pallas_call(last_kernel, in_specs=[IN_VMEM] + [ANYWHERE] * 6 + [IN_VME...  7.19 us
    pallas_call x1, Pallas kernels, per_device(): pl.pallas_call(first_kernel, in_specs=[pl.BlockSpec(memory_space=pltpu.SM...  5.56 us
    pallas_call x1, Pallas kernels, per_device(): pl.pallas_call(second_kernel, in_specs=[IN_VMEM] * 3 + [ANYWHERE, IN_VMEM...  4.06 us
    ppermute x1, starting transfers between devices, per_device(): other_grad = lax.ppermute(out_grad, 'head', [(0, 1), (1, 0)])  1.5 us
  transfers between devices with their start and end apart: 3, of which 0 were waited for; matrix products, arithmetic and copies ran while one was open for 0% of the time, Pallas kernels for 37%

profile of v5, /device:TPU:1, one launch (start us, length us, event | category | flops | bytes accessed | tf_op | source)
XLA Modules:
  0.0 59.4 jit_solution(10744515531842928557)
XLA Ops:
  0.6 1.5 %collective-permute-start = (bf16[1024,1024]{1,0:T(8,128)(2,1)}, bf16[1024,1024]{1,0:T(8,128)(2,1)S(1)}, u32[]{:S(2)}, u32[]{:S(2)}) collective-permute-start(bf16[1024,1024]{1,0:T(8,128)(2,1)} %grad_hbm.1), channel_id=1, source_target_pairs={{0,1},{1,0},{2,3},{3,2},{4,5},{5,4},{6,7},{7,6},{8,9},{9,8},{10,11... | collective-permute-start | bytes 6291464 | tf_op jit(solution)/shard_map/ppermute | solution.py:226
  2.1 5.6 %own_part.1 = (f32[1024,1024]{1,0:T(8,128)S(1)}, bf16[64,16,128]{2,1,0:T(8,128)(2,1)S(1)}, bf16[1024,1024]{1,0:T(8,128)(2,1)S(1)}) custom-call(s32[1]{0:T(128)} %bitcast.mine_ref, bf16[1024,1024]{1,0:T(8,128)(2,1)} %grad_hbm.1, bf16[1024,2048]{1,0:T(8,128)(2,1)} %weight_hbm.1, bf16[1024,1024]{1,0:T(8,128)(2,1)} %key_hbm.3, bf16[1024,1024]{1,0:T(8,128)(2,1)} %value_hbm.3), custom_call_target="tpu_custom_call" | custom-call | flops 4294967296 | bytes 12582912 | tf_op jit(solution)/shard_map/own_part/pallas_call | solution.py:231
  7.7 0.0 collective-permute-done.grad_ref
  7.7 4.1 %other_part.1 = (bf16[1024,1024]{1,0:T(8,128)(2,1)}, bf16[64,2,16,128]{3,2,1,0:T(8,128)(2,1)}) custom-call(bf16[1024,1024]{1,0:T(8,128)(2,1)S(1)} %collective-permute-done.grad_ref, bf16[1024,1024]{1,0:T(8,128)(2,1)S(1)} %get-tuple-element.14.weight_ref, f32[1024,1024]{1,0:T(8,128)S(1)} %get-tuple-element.15.part_ref, bf16[1024,1024]{1,0:T(8,128)(2,1)} %query_ref.3, ...), custom_call_target="tpu_custom_call" | custom-call | flops 4294967296 | bytes 8388608 | tf_op jit(solution)/shard_map/other_part/pallas_call | solution.py:246
  11.8 13.0 %all-to-all-start = ((bf16[64,2,16,128]{3,2,1,0:T(8,128)(2,1)}), bf16[64,2,16,128]{3,2,1,0:T(8,128)(2,1)S(1)}, u32[]{:S(2)}, u32[]{:S(2)}) async-start(bf16[64,2,16,128]{3,2,1,0:T(8,128)(2,1)} %get-tuple-element.17), calls=%async_computation | async-start | bytes 1048576 | tf_op jit(solution)/shard_map/all_to_all | solution.py:257
  24.8 8.4 %inner_0.1 = (bf16[1024,512]{1,0:T(8,128)(2,1)}, bf16[1024,512]{1,0:T(8,128)(2,1)}, bf16[1024,512]{1,0:T(8,128)(2,1)}) custom-call(bf16[64,16,128]{2,1,0:T(8,128)(2,1)S(1)} %get-tuple-element.16.state_ref.after_ref, bf16[1024,1024]{1,0:T(8,128)(2,1)} %query_ref.3, bf16[1024,1024]{1,0:T(8,128)(2,1)} %key_hbm.3, bf16[1024,1024]{1,0:T(8,128)(2,1)} %value_hbm.3, ...), custom_call_target="tpu_custom_call" | custom-call | flops 6442450944 | bytes 10485760 | tf_op jit(solution)/shard_map/inner_0/pallas_call | solution.py:260
  33.2 0.0 all-to-all-done.given_ref
  33.2 0.9 %sums.1.after_ref = bf16[64,2,16,128]{3,2,1,0:T(8,128)(2,1)} custom-call(bf16[64,2,16,128]{3,2,1,0:T(8,128)(2,1)S(1)} %all-to-all-done.given_ref, bf16[1024,512]{1,0:T(8,128)(2,1)} %get-tuple-element.19.after_ref.dq_a), custom_call_target="tpu_custom_call" | custom-call | tf_op jit(solution)/shard_map/sums/pallas_call | solution.py:274
  34.1 9.8 %all-to-all-start.1 = ((bf16[64,2,16,128]{3,2,1,0:T(8,128)(2,1)}), bf16[64,2,16,128]{3,2,1,0:T(8,128)(2,1)S(1)}, u32[]{:S(2)}, u32[]{:S(2)}) async-start(bf16[64,2,16,128]{3,2,1,0:T(8,128)(2,1)} %sums.1.after_ref), calls=%async_computation.1 | async-start | bytes 1048576 | tf_op jit(solution)/shard_map/all_to_all | solution.py:283
  43.9 8.2 %inner_4.1 = (bf16[1024,512]{1,0:T(8,128)(2,1)S(1)}, bf16[1024,512]{1,0:T(8,128)(2,1)S(1)}, bf16[1024,512]{1,0:T(8,128)(2,1)}) custom-call(bf16[64,2,16,128]{3,2,1,0:T(8,128)(2,1)} %sums.1.after_ref, bf16[1024,1024]{1,0:T(8,128)(2,1)} %query_ref.3, bf16[1024,1024]{1,0:T(8,128)(2,1)} %key_hbm.3, bf16[1024,1024]{1,0:T(8,128)(2,1)} %value_hbm.3, ...), custom_call_target="tpu_custom_call" | custom-call | flops 6442450944 | bytes 10485760 | tf_op jit(solution)/shard_map/inner_4/pallas_call | solution.py:260
  52.1 0.0 all-to-all-done.1.carried_ref
  52.1 7.2 %carried_part.1 = (bf16[1024,1024]{1,0:T(8,128)(2,1)}, bf16[1024,1024]{1,0:T(8,128)(2,1)}, bf16[1024,1024]{1,0:T(8,128)(2,1)}) custom-call(bf16[64,2,16,128]{3,2,1,0:T(8,128)(2,1)S(1)} %all-to-all-done.1.carried_ref, bf16[1024,1024]{1,0:T(8,128)(2,1)} %key_hbm.3, bf16[1024,1024]{1,0:T(8,128)(2,1)} %value_hbm.3, ...), custom_call_target="tpu_custom_call" | custom-call | flops 2147483648 | bytes 18874368 | tf_op jit(solution)/shard_map/carried_part/pallas_call | solution.py:287
Async XLA Ops:
  0.6 7.1 %collective-permute-start = (bf16[1024,1024]{1,0:T(8,128)(2,1)}, bf16[1024,1024]{1,0:T(8,128)(2,1)S(1)}, u32[]{:S(2)}, u32[]{:S(2)}) collective-permute-start(bf16[1024,1024]{1,0:T(8,128)(2,1)} %grad_hbm.1), channel_id=1, source_target_pairs={{0,1},{1,0},{2,3},{3,2},{4,5},{5,4},{6,7},{7,6},{8,9},{9,8},{10,11... | collective-permute-start | bytes 6291464 | tf_op jit(solution)/shard_map/ppermute | solution.py:226
  11.8 21.4 %all-to-all-start = ((bf16[64,2,16,128]{3,2,1,0:T(8,128)(2,1)}), bf16[64,2,16,128]{3,2,1,0:T(8,128)(2,1)S(1)}, u32[]{:S(2)}, u32[]{:S(2)}) async-start(bf16[64,2,16,128]{3,2,1,0:T(8,128)(2,1)} %get-tuple-element.17), calls=%async_computation | async-start | bytes 1048576 | tf_op jit(solution)/shard_map/all_to_all | solution.py:257
  34.1 17.9 %all-to-all-start.1 = ((bf16[64,2,16,128]{3,2,1,0:T(8,128)(2,1)}), bf16[64,2,16,128]{3,2,1,0:T(8,128)(2,1)S(1)}, u32[]{:S(2)}, u32[]{:S(2)}) async-start(bf16[64,2,16,128]{3,2,1,0:T(8,128)(2,1)} %sums.1.after_ref), calls=%async_computation.1 | async-start | bytes 1048576 | tf_op jit(solution)/shard_map/all_to_all | solution.py:283

commit v6 on v5

--- a/solution.py
+++ b/solution.py
@@ -3,6 +3,7 @@
 
 import jax
 import jax.numpy as jnp
+import numpy as np
 from jax import lax
 from jax.experimental import pallas as pl
 from jax.experimental.pallas import tpu as pltpu
@@ -103,8 +104,9 @@
         copy.wait()
 
 
-def inner_kernel(factor, after_ref, query_ref, key_ref, value_ref, head_ref, dq_ref, dk_ref, dv_ref, before_ref, behind_ref):
+def inner_kernel(factor, after_ref, query_ref, key_ref, value_ref, head_ref, dq_ref, dk_ref, dv_ref, *refs):
     del after_ref
+    *rest, before_ref, behind_ref = refs
     blocks = query_ref.shape[0] // BLOCK
     down = lax.broadcasted_iota(jnp.int32, (BLOCK, BLOCK), 0)
     across = lax.broadcasted_iota(jnp.int32, (BLOCK, BLOCK), 1)
@@ -147,20 +149,20 @@
                 if extra is not None:
                     value = value + extra[:, col]
                 out = col if ref.shape[1] == PAIR else columns(2 * pl.program_id(0) + h, HEAD)
-                ref[at, out] = value.astype(BF16)
-
-
-def middle_kernel(factor, given_ref, after_ref, carried_ref):
+                value, inside = value.astype(BF16), min(BLOCK, ref.shape[0] - b * BLOCK)
+                ref[pl.ds(b * BLOCK, inside), out] = value[:inside]
+                if inside < BLOCK:
+                    rest[0][:, col] = value[inside:]
+
+
+def middle_kernel(factor, place, given_ref, after_ref, carried_ref):
     del after_ref
     count, _, rows, width = given_ref.shape
-    total = jnp.zeros((rows, width), F32)
-    for i in reversed(range(count)):
-        carried_ref[i, 0] = (factor * total).astype(BF16)
-        total = total + given_ref[i, 0].astype(F32)
-    total = jnp.zeros((rows, width), F32)
-    for i in range(count):
-        carried_ref[i, 1] = (factor * total).astype(BF16)
-        total = total + given_ref[i, 1].astype(F32)
+    for which, devices in ((0, place), (1, place[::-1])):
+        total = jnp.zeros((rows, width), F32)
+        for i in devices:
+            carried_ref[i, which] = (factor * total).astype(BF16)
+            total = total + given_ref[i, which].astype(F32)
 
 
 def two_heads(carried_ref, h, which):
@@ -171,9 +173,10 @@
     return jnp.concatenate([jnp.concatenate([one, none], 1), jnp.concatenate([none, two], 1)], 0)
 
 
-def last_kernel(carried_ref, key_hbm, value_hbm, head_hbm, dq_a, dk_a, dv_a, dq_b, dk_b, dv_b, dq_hbm, dk_hbm, dv_hbm, *refs):
+def last_kernel(carried_ref, key_hbm, value_hbm, head_hbm, dq_a, dk_a, dv_a, dq_b, dk_b, dv_b, dv_tail, dq_hbm, dk_hbm, dv_hbm, *refs):
     inputs, outputs, (sem, out_sem) = refs[:7], refs[7:10], refs[10:]
-    sources, targets = (head_hbm, dq_a, value_hbm, dk_a, key_hbm, dv_a, dv_b), (dq_hbm, dk_hbm, dv_hbm)
+    sources, targets = (head_hbm, dq_a, value_hbm, dk_a, key_hbm, dv_a), (dq_hbm, dk_hbm, dv_hbm)
+    near_rows = dv_b.shape[0]
     length, width = outputs[0].shape
     edges = [0, TILE // 2, *range(TILE // 2 + TILE, length, TILE), length]
     tiles = [pl.ds(a, b - a) for a, b in zip(edges, edges[1:])]
@@ -181,6 +184,7 @@
         [pltpu.make_async_copy(a.at[t, :], b.at[t, :], sem.at[n, i]) for n, (a, b) in enumerate(zip(sources, inputs))]
         for i, t in enumerate(tiles)
     ]
+    loads[-1].append(pltpu.make_async_copy(dv_tail, inputs[6], sem.at[6, 0]))
     stores = [
         [pltpu.make_async_copy(a.at[t, :], b.at[t, :], out_sem.at[n, i]) for n, (a, b) in enumerate(zip(outputs, targets))]
         for i, t in enumerate(tiles)
@@ -199,7 +203,8 @@
                 locals_ = dq_in[t, col], dk_in[t, col], dv_in[t, col]
             else:
                 low = slice(j * PAIR - half, (j + 1) * PAIR - half)
-                locals_ = dq_b[t, low], dk_b[t, low], dv_rest[t, low]
+                last = edges[i] == near_rows
+                locals_ = dq_b[t, low], dk_b[t, low], dv_rest[:, low] if last else dv_b[t, low]
             sums = dot(grads[t, col], before, (1, 1)), dot(values[t, col], after, (1, 1)), dot(keys[t, col], after, (1, 0))
             for ref, own, carried in zip(outputs, locals_, sums):
                 ref[t, col] = (own + carried).astype(BF16)
@@ -212,7 +217,8 @@
 def per_device(query_rows, key_rows, value_rows, out_grad, out_weight):
     length, width = query_rows.shape
     count = lax.axis_size("ctx")
-    order = [list(reversed(range(count)))]
+    order = [count - 1, *(int(i) for i in np.random.default_rng(0).permutation(count - 1))]
+    place = [order.index(i) for i in range(count)]
     heads = width // HEAD
     factor = 1.0 / math.sqrt(HEAD * length * count)
     rows = width // count
@@ -254,15 +260,22 @@
         name="other_part",
     )(*near(other_grad, there, part), *far(query_rows), *near(key_state))
 
-    given = lax.all_to_all(sent, "ctx", 0, 0, axis_index_groups=order)
-
-    def inner(base, number, after, places):
+    given = lax.all_to_all(sent, "ctx", 0, 0, axis_index_groups=[order])
+
+    def inner(base, number, after, near_rows):
+        shapes, specs = [], []
+        for top in near_rows:
+            shapes.append(pltpu.VMEM((top, number * HEAD), BF16) if top else pltpu.HBM((length, number * HEAD), BF16))
+            specs.append(IN_VMEM if top else pl.BlockSpec((length, PAIR), lambda h: (0, h)))
+        if 0 < near_rows[2] < length:
+            shapes.append(pltpu.HBM((length - near_rows[2], number * HEAD), BF16))
+            specs.append(pl.BlockSpec((length - near_rows[2], PAIR), lambda h: (0, h)))
         return pl.pallas_call(
             functools.partial(inner_kernel, factor),
             grid=(number // 2,),
             in_specs=[ANYWHERE] + [pl.BlockSpec((length, PAIR), lambda h: (0, h + base // 2))] * 4,
-            out_specs=[IN_VMEM if p is pltpu.VMEM else pl.BlockSpec((length, PAIR), lambda h: (0, h)) for p in places],
-            out_shape=[p((length, number * HEAD), BF16) for p in places],
+            out_specs=specs,
+            out_shape=shapes,
             scratch_shapes=[pltpu.VMEM((length // BLOCK, PAIR, PAIR), BF16)] * 2,
             compiler_params=params,
             cost_estimate=cost(6 * product * number / heads, 10 * area),
@@ -270,31 +283,32 @@
         )(after, *far(query_rows, key_rows, value_rows, head_grad))
 
     half = heads // 2
-    local_a = inner(0, half, key_state, [pltpu.HBM] * 3)
+    local_a = inner(0, half, key_state, (0, 0, 0))
     carried = pl.pallas_call(
-        functools.partial(middle_kernel, factor),
+        functools.partial(middle_kernel, factor, place),
         in_specs=[IN_VMEM, ANYWHERE],
         out_specs=IN_VMEM,
         out_shape=pltpu.VMEM(given.shape, BF16),
         compiler_params=pltpu.CompilerParams(vmem_limit_bytes=4 * MIB),
         name="sums",
     )(*near(given), *far(local_a[0]))
-    local_b = inner(half, heads - half, carried, [pltpu.VMEM, pltpu.VMEM, pltpu.HBM])
-    carried = lax.all_to_all(carried, "ctx", 0, 0, axis_index_groups=order)
+    local_b = inner(half, heads - half, carried, (length, length, length - TILE // 2))
+    carried = lax.all_to_all(carried, "ctx", 0, 0, axis_index_groups=[order])
 
     full, part_width = pltpu.VMEM((length, width), BF16), pltpu.VMEM((length, width // 2), BF16)
+    tail = pltpu.VMEM((TILE // 2, width // 2), BF16)
     steps = tiles + 1
     return pl.pallas_call(
         last_kernel,
-        in_specs=[IN_VMEM] + [ANYWHERE] * 6 + [IN_VMEM] * 2 + [ANYWHERE],
+        in_specs=[IN_VMEM] + [ANYWHERE] * 6 + [IN_VMEM] * 3 + [ANYWHERE],
         out_specs=[ANYWHERE] * 3,
         out_shape=[jax.ShapeDtypeStruct((length, width), BF16)] * 3,
-        scratch_shapes=[full, part_width, full, part_width, full, part_width, part_width, full, full, full]
+        scratch_shapes=[full, part_width, full, part_width, full, part_width, tail, full, full, full]
         + [semaphores((7, steps)), semaphores((3, steps))],
         compiler_params=pltpu.CompilerParams(vmem_limit_bytes=24 * MIB),
         cost_estimate=cost(product, 18 * area),
         name="carried_part",
-    )(*near(carried), *far(key_rows, value_rows, head_grad, *local_a), *near(*local_b[:2]), *far(local_b[2]))
+    )(*near(carried), *far(key_rows, value_rows, head_grad, *local_a), *near(*local_b[:3]), *far(local_b[3]))
 
 
 def solution(mesh):

time: 59.7 us -> 58.9 us (0.987)
  no operation moved by 1% of the time
where the time goes in v6:
time: 58.9 us; the launch traced here: 58.6 us
  Pallas kernels  33.8 us (57%)
  starting transfers between devices  23.9 us (41%)
  between operations  0.83 us (1%)
    pallas_call x2, Pallas kernels, inner(): pl.pallas_call(functools.partial(inner_kernel, factor), grid=(number // 2...  16.4 us
    all_to_all x1, starting transfers between devices, per_device(): given = lax.all_to_all(sent, 'ctx', 0, 0, axis_index_groups=[order])  12.8 us
    all_to_all x1, starting transfers between devices, per_device(): carried = lax.all_to_all(carried, 'ctx', 0, 0, axis_index_groups=[order])  9.67 us
    pallas_call x1, Pallas kernels, per_device(): pl.pallas_call(last_kernel, in_specs=[IN_VMEM] + [ANYWHERE] * 6 + [IN_VME...  6.93 us
    pallas_call x1, Pallas kernels, per_device(): pl.pallas_call(first_kernel, in_specs=[pl.BlockSpec(memory_space=pltpu.SM...  5.56 us
    pallas_call x1, Pallas kernels, per_device(): pl.pallas_call(second_kernel, in_specs=[IN_VMEM] * 3 + [ANYWHERE, IN_VMEM...  4.06 us
    ppermute x1, starting transfers between devices, per_device(): other_grad = lax.ppermute(out_grad, 'head', [(0, 1), (1, 0)])  1.5 us
  transfers between devices with their start and end apart: 3, of which 0 were waited for; matrix products, arithmetic and copies ran while one was open for 0% of the time, Pallas kernels for 37%

profile of v6, /device:TPU:1, one launch (start us, length us, event | category | flops | bytes accessed | tf_op | source)
XLA Modules:
  0.0 58.6 jit_solution(13112459214353444440)
XLA Ops:
  0.6 1.5 %collective-permute-start = (bf16[1024,1024]{1,0:T(8,128)(2,1)}, bf16[1024,1024]{1,0:T(8,128)(2,1)S(1)}, u32[]{:S(2)}, u32[]{:S(2)}) collective-permute-start(bf16[1024,1024]{1,0:T(8,128)(2,1)} %grad_hbm.1), channel_id=1, source_target_pairs={{0,1},{1,0},{2,3},{3,2},{4,5},{5,4},{6,7},{7,6},{8,9},{9,8},{10,11... | collective-permute-start | bytes 6291464 | tf_op jit(solution)/shard_map/ppermute | solution.py:232
  2.1 5.6 %own_part.1 = (f32[1024,1024]{1,0:T(8,128)S(1)}, bf16[64,16,128]{2,1,0:T(8,128)(2,1)S(1)}, bf16[1024,1024]{1,0:T(8,128)(2,1)S(1)}) custom-call(s32[1]{0:T(128)} %bitcast.mine_ref, bf16[1024,1024]{1,0:T(8,128)(2,1)} %grad_hbm.1, bf16[1024,2048]{1,0:T(8,128)(2,1)} %weight_hbm.1, bf16[1024,1024]{1,0:T(8,128)(2,1)} %key_hbm.3, bf16[1024,1024]{1,0:T(8,128)(2,1)} %value_hbm.3), custom_call_target="tpu_custom_call" | custom-call | flops 4294967296 | bytes 12582912 | tf_op jit(solution)/shard_map/own_part/pallas_call | solution.py:237
  7.7 0.0 collective-permute-done.grad_ref
  7.7 4.1 %other_part.1 = (bf16[1024,1024]{1,0:T(8,128)(2,1)}, bf16[64,2,16,128]{3,2,1,0:T(8,128)(2,1)}) custom-call(bf16[1024,1024]{1,0:T(8,128)(2,1)S(1)} %collective-permute-done.grad_ref, bf16[1024,1024]{1,0:T(8,128)(2,1)S(1)} %get-tuple-element.15.weight_ref, f32[1024,1024]{1,0:T(8,128)S(1)} %get-tuple-element.16.part_ref, bf16[1024,1024]{1,0:T(8,128)(2,1)} %query_ref.3, ...), custom_call_target="tpu_custom_call" | custom-call | flops 4294967296 | bytes 8388608 | tf_op jit(solution)/shard_map/other_part/pallas_call | solution.py:252
  11.8 12.8 %all-to-all-start = ((bf16[64,2,16,128]{3,2,1,0:T(8,128)(2,1)}), bf16[64,2,16,128]{3,2,1,0:T(8,128)(2,1)S(1)}, u32[]{:S(2)}, u32[]{:S(2)}) async-start(bf16[64,2,16,128]{3,2,1,0:T(8,128)(2,1)} %get-tuple-element.18), calls=%async_computation | async-start | bytes 1048576 | tf_op jit(solution)/shard_map/all_to_all | solution.py:263
  24.6 8.4 %inner_0.1 = (bf16[1024,512]{1,0:T(8,128)(2,1)}, bf16[1024,512]{1,0:T(8,128)(2,1)}, bf16[1024,512]{1,0:T(8,128)(2,1)}) custom-call(bf16[64,16,128]{2,1,0:T(8,128)(2,1)S(1)} %get-tuple-element.17.state_ref.after_ref, bf16[1024,1024]{1,0:T(8,128)(2,1)} %query_ref.3, bf16[1024,1024]{1,0:T(8,128)(2,1)} %key_hbm.3, bf16[1024,1024]{1,0:T(8,128)(2,1)} %value_hbm.3, ...), custom_call_target="tpu_custom_call" | custom-call | flops 6442450944 | bytes 10485760 | tf_op jit(solution)/shard_map/inner_0/pallas_call | solution.py:273
  33.0 0.0 all-to-all-done.given_ref
  33.0 0.9 %sums.1.after_ref = bf16[64,2,16,128]{3,2,1,0:T(8,128)(2,1)} custom-call(bf16[64,2,16,128]{3,2,1,0:T(8,128)(2,1)S(1)} %all-to-all-done.given_ref, bf16[1024,512]{1,0:T(8,128)(2,1)} %get-tuple-element.20.after_ref.dq_a), custom_call_target="tpu_custom_call" | custom-call | tf_op jit(solution)/shard_map/sums/pallas_call | solution.py:287
  33.9 9.7 %all-to-all-start.1 = ((bf16[64,2,16,128]{3,2,1,0:T(8,128)(2,1)}), bf16[64,2,16,128]{3,2,1,0:T(8,128)(2,1)S(1)}, u32[]{:S(2)}, u32[]{:S(2)}) async-start(bf16[64,2,16,128]{3,2,1,0:T(8,128)(2,1)} %sums.1.after_ref), calls=%async_computation.1 | async-start | bytes 1048576 | tf_op jit(solution)/shard_map/all_to_all | solution.py:296
  43.6 8.0 %inner_4.1 = (bf16[1024,512]{1,0:T(8,128)(2,1)S(1)}, bf16[1024,512]{1,0:T(8,128)(2,1)S(1)}, bf16[896,512]{1,0:T(8,128)(2,1)S(1)}, bf16[128,512]{1,0:T(8,128)(2,1)}) custom-call(bf16[64,2,16,128]{3,2,1,0:T(8,128)(2,1)} %sums.1.after_ref, bf16[1024,1024]{1,0:T(8,128)(2,1)} %query_ref.3, bf16[1024,1024]{1,0:T(8,128)(2,1)} %key_hbm.3, ...), custom_call_target="tpu_custom_call" | custom-call | flops 6442450944 | bytes 10485760 | tf_op jit(solution)/shard_map/inner_4/pallas_call | solution.py:273
  51.5 0.0 all-to-all-done.1.carried_ref
  51.5 6.9 %carried_part.1 = (bf16[1024,1024]{1,0:T(8,128)(2,1)}, bf16[1024,1024]{1,0:T(8,128)(2,1)}, bf16[1024,1024]{1,0:T(8,128)(2,1)}) custom-call(bf16[64,2,16,128]{3,2,1,0:T(8,128)(2,1)S(1)} %all-to-all-done.1.carried_ref, bf16[1024,1024]{1,0:T(8,128)(2,1)} %key_hbm.3, bf16[1024,1024]{1,0:T(8,128)(2,1)} %value_hbm.3, ...), custom_call_target="tpu_custom_call" | custom-call | flops 2147483648 | bytes 18874368 | tf_op jit(solution)/shard_map/carried_part/pallas_call | solution.py:301
Async XLA Ops:
  0.6 7.1 %collective-permute-start = (bf16[1024,1024]{1,0:T(8,128)(2,1)}, bf16[1024,1024]{1,0:T(8,128)(2,1)S(1)}, u32[]{:S(2)}, u32[]{:S(2)}) collective-permute-start(bf16[1024,1024]{1,0:T(8,128)(2,1)} %grad_hbm.1), channel_id=1, source_target_pairs={{0,1},{1,0},{2,3},{3,2},{4,5},{5,4},{6,7},{7,6},{8,9},{9,8},{10,11... | collective-permute-start | bytes 6291464 | tf_op jit(solution)/shard_map/ppermute | solution.py:232
  11.8 21.2 %all-to-all-start = ((bf16[64,2,16,128]{3,2,1,0:T(8,128)(2,1)}), bf16[64,2,16,128]{3,2,1,0:T(8,128)(2,1)S(1)}, u32[]{:S(2)}, u32[]{:S(2)}) async-start(bf16[64,2,16,128]{3,2,1,0:T(8,128)(2,1)} %get-tuple-element.18), calls=%async_computation | async-start | bytes 1048576 | tf_op jit(solution)/shard_map/all_to_all | solution.py:263
  33.9 17.6 %all-to-all-start.1 = ((bf16[64,2,16,128]{3,2,1,0:T(8,128)(2,1)}), bf16[64,2,16,128]{3,2,1,0:T(8,128)(2,1)S(1)}, u32[]{:S(2)}, u32[]{:S(2)}) async-start(bf16[64,2,16,128]{3,2,1,0:T(8,128)(2,1)} %sums.1.after_ref), calls=%async_computation.1 | async-start | bytes 1048576 | tf_op jit(solution)/shard_map/all_to_all | solution.py:296

commit v7 on v6

--- a/solution.py
+++ b/solution.py
@@ -195,21 +195,24 @@
     half = width // 2
     grads, dq_in, values, dk_in, keys, dv_in, dv_rest = inputs
     for i, t in enumerate(tiles):
-        for copy in loads[i]:
-            copy.wait()
-        for j, (before, after) in enumerate(states):
-            col = slice(j * PAIR, (j + 1) * PAIR)
-            if j * PAIR < half:
-                locals_ = dq_in[t, col], dk_in[t, col], dv_in[t, col]
-            else:
-                low = slice(j * PAIR - half, (j + 1) * PAIR - half)
-                last = edges[i] == near_rows
-                locals_ = dq_b[t, low], dk_b[t, low], dv_rest[:, low] if last else dv_b[t, low]
-            sums = dot(grads[t, col], before, (1, 1)), dot(values[t, col], after, (1, 1)), dot(keys[t, col], after, (1, 0))
-            for ref, own, carried in zip(outputs, locals_, sums):
-                ref[t, col] = (own + carried).astype(BF16)
-        for copy in stores[i]:
-            copy.start()
+        last = edges[i] == near_rows
+        results = (
+            (grads, dq_in, dq_b, 0, 1, loads[i][:2]),
+            (values, dk_in, dk_b, 1, 1, loads[i][2:4]),
+            (keys, dv_in, dv_rest if last else dv_b, 1, 0, loads[i][4:]),
+        )
+        for n, (rows, own_a, own_b, which, side, needed) in enumerate(results):
+            for copy in needed:
+                copy.wait()
+            for j, pair in enumerate(states):
+                col = slice(j * PAIR, (j + 1) * PAIR)
+                if j * PAIR < half:
+                    own = own_a[t, col]
+                else:
+                    low = slice(j * PAIR - half, (j + 1) * PAIR - half)
+                    own = own_b[:, low] if own_b is dv_rest else own_b[t, low]
+                outputs[n][t, col] = (own + dot(rows[t, col], pair[which], (1, side))).astype(BF16)
+            stores[i][n].start()
     for copy in sum(stores, []):
         copy.wait()
 

time: 58.9 us -> 58.8 us (level)
  no operation moved by 1% of the time
where the time goes in v7:
time: 58.8 us; the launch traced here: 58.5 us
  Pallas kernels  33.7 us (57%)
  starting transfers between devices  23.9 us (41%)
  between operations  0.83 us (1%)
    pallas_call x2, Pallas kernels, inner(): pl.pallas_call(functools.partial(inner_kernel, factor), grid=(number // 2...  16.4 us
    all_to_all x1, starting transfers between devices, per_device(): given = lax.all_to_all(sent, 'ctx', 0, 0, axis_index_groups=[order])  12.8 us
    all_to_all x1, starting transfers between devices, per_device(): carried = lax.all_to_all(carried, 'ctx', 0, 0, axis_index_groups=[order])  9.67 us
    pallas_call x1, Pallas kernels, per_device(): pl.pallas_call(last_kernel, in_specs=[IN_VMEM] + [ANYWHERE] * 6 + [IN_VME...  6.81 us
    pallas_call x1, Pallas kernels, per_device(): pl.pallas_call(first_kernel, in_specs=[pl.BlockSpec(memory_space=pltpu.SM...  5.56 us
    pallas_call x1, Pallas kernels, per_device(): pl.pallas_call(second_kernel, in_specs=[IN_VMEM] * 3 + [ANYWHERE, IN_VMEM...  4.06 us
    ppermute x1, starting transfers between devices, per_device(): other_grad = lax.ppermute(out_grad, 'head', [(0, 1), (1, 0)])  1.5 us
  transfers between devices with their start and end apart: 3, of which 0 were waited for; matrix products, arithmetic and copies ran while one was open for 0% of the time, Pallas kernels for 37%

profile of v7, /device:TPU:1, one launch (start us, length us, event | category | flops | bytes accessed | tf_op | source)
XLA Modules:
  0.0 58.5 jit_solution(4332039460550297917)
XLA Ops:
  0.6 1.5 %collective-permute-start = (bf16[1024,1024]{1,0:T(8,128)(2,1)}, bf16[1024,1024]{1,0:T(8,128)(2,1)S(1)}, u32[]{:S(2)}, u32[]{:S(2)}) collective-permute-start(bf16[1024,1024]{1,0:T(8,128)(2,1)} %grad_hbm.1), channel_id=1, source_target_pairs={{0,1},{1,0},{2,3},{3,2},{4,5},{5,4},{6,7},{7,6},{8,9},{9,8},{10,11... | collective-permute-start | bytes 6291464 | tf_op jit(solution)/shard_map/ppermute | solution.py:235
  2.1 5.6 %own_part.1 = (f32[1024,1024]{1,0:T(8,128)S(1)}, bf16[64,16,128]{2,1,0:T(8,128)(2,1)S(1)}, bf16[1024,1024]{1,0:T(8,128)(2,1)S(1)}) custom-call(s32[1]{0:T(128)} %bitcast.mine_ref, bf16[1024,1024]{1,0:T(8,128)(2,1)} %grad_hbm.1, bf16[1024,2048]{1,0:T(8,128)(2,1)} %weight_hbm.1, bf16[1024,1024]{1,0:T(8,128)(2,1)} %key_hbm.3, bf16[1024,1024]{1,0:T(8,128)(2,1)} %value_hbm.3), custom_call_target="tpu_custom_call" | custom-call | flops 4294967296 | bytes 12582912 | tf_op jit(solution)/shard_map/own_part/pallas_call | solution.py:240
  7.7 0.0 collective-permute-done.grad_ref
  7.7 4.1 %other_part.1 = (bf16[1024,1024]{1,0:T(8,128)(2,1)}, bf16[64,2,16,128]{3,2,1,0:T(8,128)(2,1)}) custom-call(bf16[1024,1024]{1,0:T(8,128)(2,1)S(1)} %collective-permute-done.grad_ref, bf16[1024,1024]{1,0:T(8,128)(2,1)S(1)} %get-tuple-element.15.weight_ref, f32[1024,1024]{1,0:T(8,128)S(1)} %get-tuple-element.16.part_ref, bf16[1024,1024]{1,0:T(8,128)(2,1)} %query_ref.3, ...), custom_call_target="tpu_custom_call" | custom-call | flops 4294967296 | bytes 8388608 | tf_op jit(solution)/shard_map/other_part/pallas_call | solution.py:255
  11.8 12.8 %all-to-all-start = ((bf16[64,2,16,128]{3,2,1,0:T(8,128)(2,1)}), bf16[64,2,16,128]{3,2,1,0:T(8,128)(2,1)S(1)}, u32[]{:S(2)}, u32[]{:S(2)}) async-start(bf16[64,2,16,128]{3,2,1,0:T(8,128)(2,1)} %get-tuple-element.18), calls=%async_computation | async-start | bytes 1048576 | tf_op jit(solution)/shard_map/all_to_all | solution.py:266
  24.6 8.4 %inner_0.1 = (bf16[1024,512]{1,0:T(8,128)(2,1)}, bf16[1024,512]{1,0:T(8,128)(2,1)}, bf16[1024,512]{1,0:T(8,128)(2,1)}) custom-call(bf16[64,16,128]{2,1,0:T(8,128)(2,1)S(1)} %get-tuple-element.17.state_ref.after_ref, bf16[1024,1024]{1,0:T(8,128)(2,1)} %query_ref.3, bf16[1024,1024]{1,0:T(8,128)(2,1)} %key_hbm.3, bf16[1024,1024]{1,0:T(8,128)(2,1)} %value_hbm.3, ...), custom_call_target="tpu_custom_call" | custom-call | flops 6442450944 | bytes 10485760 | tf_op jit(solution)/shard_map/inner_0/pallas_call | solution.py:276
  33.0 0.0 all-to-all-done.given_ref
  33.0 0.9 %sums.1.after_ref = bf16[64,2,16,128]{3,2,1,0:T(8,128)(2,1)} custom-call(bf16[64,2,16,128]{3,2,1,0:T(8,128)(2,1)S(1)} %all-to-all-done.given_ref, bf16[1024,512]{1,0:T(8,128)(2,1)} %get-tuple-element.20.after_ref.dq_a), custom_call_target="tpu_custom_call" | custom-call | tf_op jit(solution)/shard_map/sums/pallas_call | solution.py:290
  33.9 9.7 %all-to-all-start.1 = ((bf16[64,2,16,128]{3,2,1,0:T(8,128)(2,1)}), bf16[64,2,16,128]{3,2,1,0:T(8,128)(2,1)S(1)}, u32[]{:S(2)}, u32[]{:S(2)}) async-start(bf16[64,2,16,128]{3,2,1,0:T(8,128)(2,1)} %sums.1.after_ref), calls=%async_computation.1 | async-start | bytes 1048576 | tf_op jit(solution)/shard_map/all_to_all | solution.py:299
  43.6 8.0 %inner_4.1 = (bf16[1024,512]{1,0:T(8,128)(2,1)S(1)}, bf16[1024,512]{1,0:T(8,128)(2,1)S(1)}, bf16[896,512]{1,0:T(8,128)(2,1)S(1)}, bf16[128,512]{1,0:T(8,128)(2,1)}) custom-call(bf16[64,2,16,128]{3,2,1,0:T(8,128)(2,1)} %sums.1.after_ref, bf16[1024,1024]{1,0:T(8,128)(2,1)} %query_ref.3, bf16[1024,1024]{1,0:T(8,128)(2,1)} %key_hbm.3, ...), custom_call_target="tpu_custom_call" | custom-call | flops 6442450944 | bytes 10485760 | tf_op jit(solution)/shard_map/inner_4/pallas_call | solution.py:276
  51.5 0.0 all-to-all-done.1.carried_ref
  51.5 6.8 %carried_part.1 = (bf16[1024,1024]{1,0:T(8,128)(2,1)}, bf16[1024,1024]{1,0:T(8,128)(2,1)}, bf16[1024,1024]{1,0:T(8,128)(2,1)}) custom-call(bf16[64,2,16,128]{3,2,1,0:T(8,128)(2,1)S(1)} %all-to-all-done.1.carried_ref, bf16[1024,1024]{1,0:T(8,128)(2,1)} %key_hbm.3, bf16[1024,1024]{1,0:T(8,128)(2,1)} %value_hbm.3, ...), custom_call_target="tpu_custom_call" | custom-call | flops 2147483648 | bytes 18874368 | tf_op jit(solution)/shard_map/carried_part/pallas_call | solution.py:304
Async XLA Ops:
  0.6 7.1 %collective-permute-start = (bf16[1024,1024]{1,0:T(8,128)(2,1)}, bf16[1024,1024]{1,0:T(8,128)(2,1)S(1)}, u32[]{:S(2)}, u32[]{:S(2)}) collective-permute-start(bf16[1024,1024]{1,0:T(8,128)(2,1)} %grad_hbm.1), channel_id=1, source_target_pairs={{0,1},{1,0},{2,3},{3,2},{4,5},{5,4},{6,7},{7,6},{8,9},{9,8},{10,11... | collective-permute-start | bytes 6291464 | tf_op jit(solution)/shard_map/ppermute | solution.py:235
  11.8 21.2 %all-to-all-start = ((bf16[64,2,16,128]{3,2,1,0:T(8,128)(2,1)}), bf16[64,2,16,128]{3,2,1,0:T(8,128)(2,1)S(1)}, u32[]{:S(2)}, u32[]{:S(2)}) async-start(bf16[64,2,16,128]{3,2,1,0:T(8,128)(2,1)} %get-tuple-element.18), calls=%async_computation | async-start | bytes 1048576 | tf_op jit(solution)/shard_map/all_to_all | solution.py:266
  33.9 17.6 %all-to-all-start.1 = ((bf16[64,2,16,128]{3,2,1,0:T(8,128)(2,1)}), bf16[64,2,16,128]{3,2,1,0:T(8,128)(2,1)S(1)}, u32[]{:S(2)}, u32[]{:S(2)}) async-start(bf16[64,2,16,128]{3,2,1,0:T(8,128)(2,1)} %sums.1.after_ref), calls=%async_computation.1 | async-start | bytes 1048576 | tf_op jit(solution)/shard_map/all_to_all | solution.py:299

commit v8 on v7

--- a/solution.py
+++ b/solution.py
@@ -83,7 +83,8 @@
     rest.wait()
 
 
-def second_kernel(grad_ref, weight_ref, part_ref, query_hbm, state_ref, head_hbm, sent_ref, query_ref, head_ref, sem, query_sem):
+def second_kernel(grad_ref, weight_ref, part_ref, query_hbm, state_ref, head_hbm, sent_hbm,
+                  query_ref, head_ref, sent_ref, sem, query_sem, sent_sem):
     rows = state_ref.shape[1]
     each = HEAD // rows
     fetch = pltpu.make_async_copy(query_hbm, query_ref, query_sem)
@@ -97,6 +98,10 @@
 
     def write(h, state):
         sent_ref[h * each : (h + 1) * each, 1] = state.reshape(each, rows, HEAD)
+        if h % 2:
+            both = pl.ds((h - 1) * each, 2 * each)
+            copies.append(pltpu.make_async_copy(sent_ref.at[both], sent_hbm.at[both], sent_sem.at[h // 2]))
+            copies[-1].start()
 
     fetch.wait()
     put_states(query_ref, head_ref, write)
@@ -255,9 +260,11 @@
     head_grad, sent = pl.pallas_call(
         second_kernel,
         in_specs=[IN_VMEM] * 3 + [ANYWHERE, IN_VMEM],
-        out_specs=[ANYWHERE, IN_VMEM],
-        out_shape=[pltpu.HBM((length, width), BF16), pltpu.VMEM((count, 2, rows, HEAD), BF16)],
-        scratch_shapes=[pltpu.VMEM((length, width), BF16)] * 2 + [semaphores((tiles,)), semaphores],
+        out_specs=[ANYWHERE, ANYWHERE],
+        out_shape=[pltpu.HBM((length, width), BF16), pltpu.HBM((count, 2, rows, HEAD), BF16)],
+        scratch_shapes=[pltpu.VMEM((length, width), BF16)] * 2
+        + [pltpu.VMEM((count, 2, rows, HEAD), BF16)]
+        + [semaphores((tiles,)), semaphores, semaphores((heads // 2,))],
         compiler_params=params,
         cost_estimate=cost(2 * product, 8 * area),
         name="other_part",

time: 58.8 us -> 58.6 us (level)
  transfers between devices with their start and end apart: 3 -> 3, of which waited for: 0 -> 0; matrix products, arithmetic and copies ran while one was open for 0% -> 0% of each run, Pallas kernels for 37% -> 38%
where the time goes in v8:
time: 58.6 us; the launch traced here: 58.4 us
  Pallas kernels  33.6 us (57%)
  starting transfers between devices  24 us (41%)
  between operations  0.83 us (1%)
    pallas_call x2, Pallas kernels, inner(): pl.pallas_call(functools.partial(inner_kernel, factor), grid=(number // 2...  16.4 us
    all_to_all x1, starting transfers between devices, per_device(): given = lax.all_to_all(sent, 'ctx', 0, 0, axis_index_groups=[order])  12.8 us
    all_to_all x1, starting transfers between devices, per_device(): carried = lax.all_to_all(carried, 'ctx', 0, 0, axis_index_groups=[order])  9.69 us
    pallas_call x1, Pallas kernels, per_device(): pl.pallas_call(last_kernel, in_specs=[IN_VMEM] + [ANYWHERE] * 6 + [IN_VME...  6.81 us
    pallas_call x1, Pallas kernels, per_device(): pl.pallas_call(first_kernel, in_specs=[pl.BlockSpec(memory_space=pltpu.SM...  5.56 us
    pallas_call x1, Pallas kernels, per_device(): pl.pallas_call(second_kernel, in_specs=[IN_VMEM] * 3 + [ANYWHERE, IN_VMEM...  3.9 us
    ppermute x1, starting transfers between devices, per_device(): other_grad = lax.ppermute(out_grad, 'head', [(0, 1), (1, 0)])  1.5 us
  transfers between devices with their start and end apart: 3, of which 0 were waited for; matrix products, arithmetic and copies ran while one was open for 0% of the time, Pallas kernels for 38%

profile of v8, /device:TPU:1, one launch (start us, length us, event | category | flops | bytes accessed | tf_op | source)
XLA Modules:
  0.0 58.4 jit_solution(7394430717259924704)
XLA Ops:
  0.6 1.5 %collective-permute-start = (bf16[1024,1024]{1,0:T(8,128)(2,1)}, bf16[1024,1024]{1,0:T(8,128)(2,1)S(1)}, u32[]{:S(2)}, u32[]{:S(2)}) collective-permute-start(bf16[1024,1024]{1,0:T(8,128)(2,1)} %grad_hbm.1), channel_id=1, source_target_pairs={{0,1},{1,0},{2,3},{3,2},{4,5},{5,4},{6,7},{7,6},{8,9},{9,8},{10,11... | collective-permute-start | bytes 6291464 | tf_op jit(solution)/shard_map/ppermute | solution.py:240
  2.1 5.6 %own_part.1 = (f32[1024,1024]{1,0:T(8,128)S(1)}, bf16[64,16,128]{2,1,0:T(8,128)(2,1)S(1)}, bf16[1024,1024]{1,0:T(8,128)(2,1)S(1)}) custom-call(s32[1]{0:T(128)} %bitcast.mine_ref, bf16[1024,1024]{1,0:T(8,128)(2,1)} %grad_hbm.1, bf16[1024,2048]{1,0:T(8,128)(2,1)} %weight_hbm.1, bf16[1024,1024]{1,0:T(8,128)(2,1)} %key_hbm.3, bf16[1024,1024]{1,0:T(8,128)(2,1)} %value_hbm.3), custom_call_target="tpu_custom_call" | custom-call | flops 4294967296 | bytes 12582912 | tf_op jit(solution)/shard_map/own_part/pallas_call | solution.py:245
  7.7 0.0 collective-permute-done.grad_ref
  7.7 3.9 %other_part.1 = (bf16[1024,1024]{1,0:T(8,128)(2,1)}, bf16[64,2,16,128]{3,2,1,0:T(8,128)(2,1)}) custom-call(bf16[1024,1024]{1,0:T(8,128)(2,1)S(1)} %collective-permute-done.grad_ref, bf16[1024,1024]{1,0:T(8,128)(2,1)S(1)} %get-tuple-element.15.weight_ref, f32[1024,1024]{1,0:T(8,128)S(1)} %get-tuple-element.16.part_ref, bf16[1024,1024]{1,0:T(8,128)(2,1)} %query_ref.3, ...), custom_call_target="tpu_custom_call" | custom-call | flops 4294967296 | bytes 8388608 | tf_op jit(solution)/shard_map/other_part/pallas_call | solution.py:260
  11.6 12.8 %all-to-all-start = ((bf16[64,2,16,128]{3,2,1,0:T(8,128)(2,1)}), bf16[64,2,16,128]{3,2,1,0:T(8,128)(2,1)S(1)}, u32[]{:S(2)}, u32[]{:S(2)}) async-start(bf16[64,2,16,128]{3,2,1,0:T(8,128)(2,1)} %get-tuple-element.18), calls=%async_computation | async-start | bytes 1048576 | tf_op jit(solution)/shard_map/all_to_all | solution.py:273
  24.4 8.4 %inner_0.1 = (bf16[1024,512]{1,0:T(8,128)(2,1)}, bf16[1024,512]{1,0:T(8,128)(2,1)}, bf16[1024,512]{1,0:T(8,128)(2,1)}) custom-call(bf16[64,16,128]{2,1,0:T(8,128)(2,1)S(1)} %get-tuple-element.17.state_ref.after_ref, bf16[1024,1024]{1,0:T(8,128)(2,1)} %query_ref.3, bf16[1024,1024]{1,0:T(8,128)(2,1)} %key_hbm.3, bf16[1024,1024]{1,0:T(8,128)(2,1)} %value_hbm.3, ...), custom_call_target="tpu_custom_call" | custom-call | flops 6442450944 | bytes 10485760 | tf_op jit(solution)/shard_map/inner_0/pallas_call | solution.py:283
  32.8 0.0 all-to-all-done.given_ref
  32.8 0.9 %sums.1.after_ref = bf16[64,2,16,128]{3,2,1,0:T(8,128)(2,1)} custom-call(bf16[64,2,16,128]{3,2,1,0:T(8,128)(2,1)S(1)} %all-to-all-done.given_ref, bf16[1024,512]{1,0:T(8,128)(2,1)} %get-tuple-element.20.after_ref.dq_a), custom_call_target="tpu_custom_call" | custom-call | tf_op jit(solution)/shard_map/sums/pallas_call | solution.py:297
  33.7 9.7 %all-to-all-start.1 = ((bf16[64,2,16,128]{3,2,1,0:T(8,128)(2,1)}), bf16[64,2,16,128]{3,2,1,0:T(8,128)(2,1)S(1)}, u32[]{:S(2)}, u32[]{:S(2)}) async-start(bf16[64,2,16,128]{3,2,1,0:T(8,128)(2,1)} %sums.1.after_ref), calls=%async_computation.1 | async-start | bytes 1048576 | tf_op jit(solution)/shard_map/all_to_all | solution.py:306
  43.4 8.0 %inner_4.1 = (bf16[1024,512]{1,0:T(8,128)(2,1)S(1)}, bf16[1024,512]{1,0:T(8,128)(2,1)S(1)}, bf16[896,512]{1,0:T(8,128)(2,1)S(1)}, bf16[128,512]{1,0:T(8,128)(2,1)}) custom-call(bf16[64,2,16,128]{3,2,1,0:T(8,128)(2,1)} %sums.1.after_ref, bf16[1024,1024]{1,0:T(8,128)(2,1)} %query_ref.3, bf16[1024,1024]{1,0:T(8,128)(2,1)} %key_hbm.3, ...), custom_call_target="tpu_custom_call" | custom-call | flops 6442450944 | bytes 10485760 | tf_op jit(solution)/shard_map/inner_4/pallas_call | solution.py:283
  51.4 0.0 all-to-all-done.1.carried_ref
  51.4 6.8 %carried_part.1 = (bf16[1024,1024]{1,0:T(8,128)(2,1)}, bf16[1024,1024]{1,0:T(8,128)(2,1)}, bf16[1024,1024]{1,0:T(8,128)(2,1)}) custom-call(bf16[64,2,16,128]{3,2,1,0:T(8,128)(2,1)S(1)} %all-to-all-done.1.carried_ref, bf16[1024,1024]{1,0:T(8,128)(2,1)} %key_hbm.3, bf16[1024,1024]{1,0:T(8,128)(2,1)} %value_hbm.3, ...), custom_call_target="tpu_custom_call" | custom-call | flops 2147483648 | bytes 18874368 | tf_op jit(solution)/shard_map/carried_part/pallas_call | solution.py:311
Async XLA Ops:
  0.6 7.1 %collective-permute-start = (bf16[1024,1024]{1,0:T(8,128)(2,1)}, bf16[1024,1024]{1,0:T(8,128)(2,1)S(1)}, u32[]{:S(2)}, u32[]{:S(2)}) collective-permute-start(bf16[1024,1024]{1,0:T(8,128)(2,1)} %grad_hbm.1), channel_id=1, source_target_pairs={{0,1},{1,0},{2,3},{3,2},{4,5},{5,4},{6,7},{7,6},{8,9},{9,8},{10,11... | collective-permute-start | bytes 6291464 | tf_op jit(solution)/shard_map/ppermute | solution.py:240
  11.6 21.2 %all-to-all-start = ((bf16[64,2,16,128]{3,2,1,0:T(8,128)(2,1)}), bf16[64,2,16,128]{3,2,1,0:T(8,128)(2,1)S(1)}, u32[]{:S(2)}, u32[]{:S(2)}) async-start(bf16[64,2,16,128]{3,2,1,0:T(8,128)(2,1)} %get-tuple-element.18), calls=%async_computation | async-start | bytes 1048576 | tf_op jit(solution)/shard_map/all_to_all | solution.py:273
  33.7 17.7 %all-to-all-start.1 = ((bf16[64,2,16,128]{3,2,1,0:T(8,128)(2,1)}), bf16[64,2,16,128]{3,2,1,0:T(8,128)(2,1)S(1)}, u32[]{:S(2)}, u32[]{:S(2)}) async-start(bf16[64,2,16,128]{3,2,1,0:T(8,128)(2,1)} %sums.1.after_ref), calls=%async_computation.1 | async-start | bytes 1048576 | tf_op jit(solution)/shard_map/all_to_all | solution.py:306
